TPU v7x, 32 devices: a whole 2x2x4 slice. The times are simulated.
32 devices in a mesh: row: 8 (over z, x), col: 4 (over y, core).
Axes of the slice: x: 2, y: 2, z: 4, core: 2. Of those that a mesh axis runs over, the one named last changes fastest.
Arguments:
- tiles: bfloat16 [8, 96, 256, 256], P('row', 'col'), may hold values from -0.109375 to 0.109375
- tile_slot: int32 [8, 96], P('row', 'col'), may hold values from 0 to 31
- tile_count: int32 [8, 4], P('row', 'col'), may hold values from 1 to 24, 48 in all within a row
- feats: bfloat16 [8192, 256], P('col'), may hold values from -6 to 6
- weight: bfloat16 [256, 256], replicated, may hold values from -0.375 to 0.375
- out_grad: bfloat16 [8192, 256], P(('row', 'col')), may hold values from -6 to 6
Outputs:
- activated: bfloat16 [8192, 256], P(('row', 'col'))
- weight_grad: float32 [256, 256], replicated
- window_grad: bfloat16 [4, 2048, 256], P('col', 'row')
Inputs may be any that keep to these rules, and one draw needn't show every extreme that they name: `tile_count`: some block in every draw has all 24 slots in use.
All inputs are finite; a program needn't handle non-finite values.
Results may differ from a plain program's by a relative error of at most 0.0065.
Values may be sent and summed in bfloat16 or wider, within the bound.
A program may use at most 64 MiB of HBM per device.

v0:
```python
import math

import jax
import jax.numpy as jnp
from jax import lax
from jax.sharding import PartitionSpec as P

RT = 4


def tile_products(blocks, source, take_index, put_index, live_count, out_tiles, transposed):
    tile_size = blocks.shape[1]
    feature_width = source.shape[2]
    initial = jnp.zeros((out_tiles, tile_size, feature_width), jnp.float32)

    def one_step(position, totals):
        one_block = lax.dynamic_index_in_dim(blocks, position, 0, False)
        source_block = lax.dynamic_index_in_dim(source, take_index[position], 0, False)
        if transposed:
            product = lax.dot_general(
                one_block,
                source_block,
                (((0,), (0,)), ((), ())),
                preferred_element_type=jnp.float32,
            )
        else:
            product = jnp.dot(one_block, source_block, preferred_element_type=jnp.float32)
        target = put_index[position]
        updated = lax.dynamic_index_in_dim(totals, target, 0, False) + product
        return lax.dynamic_update_index_in_dim(totals, updated, target, 0)

    return lax.fori_loop(0, live_count, one_step, initial)


def on_device(tiles, tile_slot, tile_count, feats, weight, out_grad):
    blocks = tiles[0]
    slots = tile_slot[0]
    live_count = tile_count[0, 0]
    tile_size = blocks.shape[1]
    feature_width = feats.shape[1]
    col_tiles = feats.shape[0] // tile_size
    col_index = slots % col_tiles
    row_index = slots // col_tiles
    feature_tiles = feats.reshape(col_tiles, tile_size, feature_width)
    row_partial = tile_products(blocks, feature_tiles, col_index, row_index, live_count, RT, False)
    row_partial = row_partial.reshape(RT * tile_size, feature_width)
    grad_scale = 1.0 / math.sqrt(RT * tile_size * lax.axis_size("row"))
    contract_rows = (((0,), (0,)), ((), ()))
    row_share = lax.psum_scatter(row_partial, "col", scatter_dimension=0, tiled=True)
    aggregated = row_share.astype(jnp.bfloat16)
    pre_act = jnp.dot(aggregated, weight, preferred_element_type=jnp.float32)
    sigmoid_pre = jax.nn.sigmoid(pre_act)
    activated = (pre_act * sigmoid_pre).astype(jnp.bfloat16)
    grad_pre = (
        out_grad.astype(jnp.float32) * sigmoid_pre * (1.0 + pre_act * (1.0 - sigmoid_pre))
    ).astype(jnp.bfloat16)
    local_grad = lax.dot_general(
        aggregated, grad_pre, contract_rows, preferred_element_type=jnp.float32
    )
    weight_grad = lax.psum(local_grad, ("row", "col")) * grad_scale
    grad_share = jnp.dot(grad_pre, weight.T, preferred_element_type=jnp.float32).astype(
        jnp.bfloat16
    )
    grad_block = lax.all_gather(grad_share, "col", axis=0, tiled=True)
    grad_tiles = grad_block.reshape(RT, tile_size, feature_width)
    col_partial = tile_products(
        blocks, grad_tiles, row_index, col_index, live_count, col_tiles, True
    )
    col_partial = col_partial.reshape(col_tiles * tile_size, feature_width)
    col_share = lax.psum_scatter(col_partial, "row", scatter_dimension=0, tiled=True)
    window_grad = col_share.astype(jnp.bfloat16)[None, :, :]
    return (activated, weight_grad, window_grad)


def solution(mesh):
    placed = (
        P("row", "col", None, None),
        P("row", "col"),
        P("row", "col"),
        P("col", None),
        P(),
        P(("row", "col"), None),
    )
    return jax.shard_map(
        on_device,
        mesh=mesh,
        in_specs=placed,
        out_specs=(P(("row", "col"), None), P(), P("col", "row", None)),
        check_vma=False,
    )
```

profile of v0, /device:TPU:0, one launch (start us, length us, event | category | flops | bytes accessed | tf_op | source)
XLA Modules:
  0.0 456.0 jit_solution(3168479342885202993)
XLA Ops:
  7.2 0.0 reduce-scatter.3.cloned.1.call-start
  7.2 0.7 and_select_fusion
  7.9 0.1 broadcast_in_dim.17
  8.0 49.2 %while.20 = (s32[]{:T(128)}, f32[4,256,256]{2,1,0:T(8,128)S(1)}, s32[]{:T(128)}, s32[24]{0:T(128)S(1)}, bf16[24,256,256]{2,1,0:T(8,128)(2,1)}, /*index=5*/s32[24...) while((s32[]{:T(128)}, f32[4,256,256]{2,1,0:T(8,128)S(1)}, ...), condition=%wide.region_1.2_spmd, body=%wide.region_0.1_spmd.sunk | while | flops 33619976 | bytes 1310987 | solution.py:32
  8.7 0.6 dynamic_slice.66
  11.2 0.6 dynamic_slice.67
  13.8 1.2 fusion.30
  15.7 0.6 dynamic_slice.66
  18.2 0.6 dynamic_slice.67
  20.7 1.2 fusion.30
  22.6 0.6 dynamic_slice.66
  25.1 0.6 dynamic_slice.67
  27.7 1.2 fusion.30
  29.5 0.6 dynamic_slice.66
  32.0 0.6 dynamic_slice.67
  34.6 1.2 fusion.30
  36.4 0.6 dynamic_slice.66
  39.0 0.6 dynamic_slice.67
  41.5 1.2 fusion.30
  43.4 0.6 dynamic_slice.66
  45.9 0.6 dynamic_slice.67
  48.5 1.2 fusion.30
  50.3 0.6 dynamic_slice.66
  52.8 0.6 dynamic_slice.67
  55.4 1.2 fusion.30
  57.2 1.0 copy-done.2
  58.2 0.0 reduce-scatter.3.cloned.1.call-update
  58.2 0.0 all-reduce.2.cloned.1.call-start
  58.3 144.1 %reduce-scatter.3.cloned.1.call-done = f32[256,256]{1,0:T(8,128)} async-done(((f32[1024,256]{1,0:T(8,128)}), f32[256,256]{1,0:T(8,128)}) %reduce-scatter.3.cloned.1.call-update) | async-done | bytes 262160 | tf_op jit(solution)/shard_map/reduce_scatter | solution.py:49
  202.3 2.0 multiply_convert_fusion
  204.3 0.2 convolution_convert_fusion
  204.5 0.9 fusion.14
  205.5 0.0 all-reduce.2.cloned.1.call-update
  205.5 0.0 reduce-scatter.5.cloned.1.call-start
  205.5 6.8 %all_gather.3 = bf16[1024,256]{1,0:T(8,128)(2,1)S(1)} all-gather(bf16[256,256]{1,0:T(8,128)(2,1)S(1)} %convolution_convert_fusion), channel_id=1, replica_groups=mesh['row'=8,'col'=4] {'col'}, dimensions={0}, use_global_device_ids=true | all-gather | bytes 655360 | tf_op jit(solution)/shard_map/all_gather | solution.py:64
  212.3 0.2 broadcast_in_dim.18
  212.5 48.9 %while.21 = (s32[]{:T(128)}, f32[8,256,256]{2,1,0:T(8,128)S(1)}, s32[]{:T(128)}, s32[24]{0:T(128)S(1)}, bf16[24,256,256]{2,1,0:T(8,128)(2,1)}, /*index=5*/s32[24...) while((s32[]{:T(128)}, f32[8,256,256]{2,1,0:T(8,128)S(1)}, ...), condition=%wide.region_5.6_spmd, body=%wide.region_4.5_spmd.sunk | while | flops 33619976 | bytes 1310987 | solution.py:32
  213.2 0.6 dynamic_slice.71
  215.7 0.6 dynamic_slice.72
  218.2 1.1 fusion.33
  220.0 0.6 dynamic_slice.71
  222.6 0.6 dynamic_slice.72
  225.1 1.1 fusion.33
  226.9 0.6 dynamic_slice.71
  229.5 0.6 dynamic_slice.72
  232.0 1.1 fusion.33
  233.8 0.6 dynamic_slice.71
  236.3 0.6 dynamic_slice.72
  238.9 1.1 fusion.33
  240.7 0.6 dynamic_slice.71
  243.2 0.6 dynamic_slice.72
  245.8 1.1 fusion.33
  247.6 0.6 dynamic_slice.71
  250.1 0.6 dynamic_slice.72
  252.7 1.1 fusion.33
  254.5 0.6 dynamic_slice.71
  257.0 0.6 dynamic_slice.72
  259.6 1.1 fusion.33
  261.4 1.3 copy-done.1
  262.7 0.0 reduce-scatter.5.cloned.1.call-update
  262.7 71.7 %all-reduce.2.cloned.1.call-done = f32[256,256]{1,0:T(8,128)} async-done(((f32[256,256]{1,0:T(8,128)}), f32[256,256]{1,0:T(8,128)}) %all-reduce.2.cloned.1.call-update) | async-done | bytes 262160 | tf_op jit(solution)/shard_map/psum | solution.py:60
  334.4 1.7 broadcast_multiply_fusion
  336.1 111.8 %reduce-scatter.5.cloned.1.call-done = f32[256,256]{1,0:T(8,128)} async-done(((f32[2048,256]{1,0:T(8,128)}), f32[256,256]{1,0:T(8,128)}) %reduce-scatter.5.cloned.1.call-update) | async-done | bytes 262160 | tf_op jit(solution)/shard_map/reduce_scatter | solution.py:70
  447.8 1.6 convert_bitcast_fusion
  (22 shorter events, 0.4 us)
Async XLA Ops:
  7.2 195.2 %copy-start = (bf16[256,256]{1,0:T(8,128)(2,1)S(1)}, bf16[256,256]{1,0:T(8,128)(2,1)}, u32[]{:S(2)}) copy-start(bf16[256,256]{1,0:T(8,128)(2,1)} %param.14) | copy-start | bytes 393220
  7.2 195.1 %reduce-scatter.3.cloned.1.call-start = ((), (), s32[]{:S(2)}) async-start(), calls=%async_computation.2 | async-start | bytes 1310720 | tf_op jit(solution)/shard_map/reduce_scatter | solution.py:49
  8.0 194.3 %copy-start.4 = (bf16[256,256]{1,0:T(8,128)(2,1)S(1)}, bf16[256,256]{1,0:T(8,128)(2,1)}, u32[]{:S(2)}) copy-start(bf16[256,256]{1,0:T(8,128)(2,1)} %param.15) | copy-start | bytes 393220
  57.2 1.0 copy-start.2
  58.2 276.2 %all-reduce.2.cloned.1.call-start = ((), (), s32[]{:S(2)}) async-start(), calls=%async_computation.3 | async-start | bytes 524288 | tf_op jit(solution)/shard_map/psum | solution.py:60
  202.3 2.2 copy-start.3
  205.5 242.4 %reduce-scatter.5.cloned.1.call-start = ((), (), s32[]{:S(2)}) async-start(), calls=%async_computation.4 | async-start | bytes 2359296 | tf_op jit(solution)/shard_map/reduce_scatter | solution.py:70
  261.4 1.3 copy-start.1
Sparse Core Ops, SparseCore 0:
  58.3 143.9 reduce-scatter.2
  209.3 125.0 all-reduce.1
  338.3 109.4 reduce-scatter.4
where the time goes:
time: 461 us; the launch traced here: 456 us
  waiting for transfers between devices  328 us (71%)
  loops' own time  64.5 us (14%)
  local copies, waits for them, and re-layouts  20.1 us (4%)
  matrix products  19.2 us (4%)
  between operations  13.8 us (3%)
  blocking collectives  6.78 us (1%)
    reduce_scatter x1, waiting for transfers between devices, on_device(): lax.psum_scatter(row_partial, 'col', scatter_dimension=0, tiled=True)  144 us
    reduce_scatter x1, waiting for transfers between devices, on_device(): lax.psum_scatter(col_partial, 'row', scatter_dimension=0, tiled=True)  112 us
    psum x1, waiting for transfers between devices, on_device(): weight_grad = lax.psum(local_grad, ('row', 'col')) * grad_scale  71.7 us
    another operation x2, loops' own time, tile_products(): return lax.fori_loop(0, live_count, one_step, initial)  64.5 us
  transfers between devices with their start and end apart: 3, of which 3 were waited for; matrix products, arithmetic and copies ran while one was open for 4% of the time, Pallas kernels for 0%

commit v1 on v0

v1 whole, which is shorter than its diff:
```python
import functools
import math

import jax
import jax.numpy as jnp
from jax import lax
from jax.experimental import pallas as pl
from jax.experimental.pallas import tpu as pltpu
from jax.sharding import PartitionSpec as P

RT = 4
LANES = 128
MESH = pl.DeviceIdType.MESH
F32 = jnp.float32
BF16 = jnp.bfloat16


def block_kernel(slots, count, tiles, feats, block, partial, dense, extra, source, total,
                 first, others, following, tile_sem, feat_sem, out_sem):
    size = tiles.shape[1]
    col_tiles = feats.shape[0] // size
    places = RT * col_tiles
    live = count[0]

    feat_copy = pltpu.make_async_copy(feats, source, feat_sem)
    feat_copy.start()

    def place_of(slot):
        row = pl.multiple_of(slot // col_tiles * size, size)
        column = pl.multiple_of(slot % col_tiles * size, size)
        return dense.at[pl.ds(row, size), pl.ds(column, size)]

    @pl.loop(0, places)
    def _(place):
        first[place] = -1
        others[place] = -1

    @pl.loop(0, live)
    def _(position):
        slot = slots[position]
        taken = first[slot] >= 0

        @pl.when(jnp.logical_not(taken))
        def _():
            first[slot] = position
            pltpu.make_async_copy(tiles.at[position], place_of(slot), tile_sem.at[position]).start()

        @pl.when(taken)
        def _():
            following[position] = others[slot]
            others[slot] = position
            pltpu.make_async_copy(
                tiles.at[position], extra.at[position], tile_sem.at[position]
            ).start()

    @pl.loop(0, places)
    def _(place):
        @pl.when(first[place] < 0)
        def _():
            place_of(place)[...] = jnp.zeros((size, size), BF16)

    def await_tile(position):
        pltpu.make_async_copy(
            tiles.at[position], extra.at[position], tile_sem.at[position]
        ).wait()

    for row in range(RT):
        @pl.loop(row * col_tiles, (row + 1) * col_tiles)
        def _(place):
            @pl.when(first[place] >= 0)
            def _():
                await_tile(first[place])

                @pl.when(others[place] >= 0)
                def _():
                    spot = place_of(place)
                    total[...] = spot[...].astype(F32)

                    def add(position):
                        await_tile(position)
                        total[...] += extra[position].astype(F32)
                        return following[position]

                    lax.while_loop(lambda position: position >= 0, add, others[place])
                    spot[...] = total[...].astype(BF16)

        rows = pl.ds(row * size, size)
        pltpu.make_async_copy(dense.at[rows], block.at[rows], out_sem.at[row]).start()
        if row == 0:
            feat_copy.wait()
        partial[rows, :] = jnp.dot(
            dense[rows, :], source[...], preferred_element_type=F32
        ).astype(BF16)

    for row in range(RT):
        rows = pl.ds(row * size, size)
        pltpu.make_async_copy(dense.at[rows], block.at[rows], out_sem.at[row]).wait()


def block_product(tiles, slots, count, feats):
    number, size, _ = tiles.shape
    window, width = feats.shape
    places = RT * window // size
    return pl.pallas_call(
        block_kernel,
        out_shape=(
            jax.ShapeDtypeStruct((RT * size, window), BF16),
            jax.ShapeDtypeStruct((RT * size, width), BF16),
        ),
        in_specs=[
            pl.BlockSpec(memory_space=pltpu.SMEM),
            pl.BlockSpec(memory_space=pltpu.SMEM),
            pl.BlockSpec(memory_space=pl.ANY),
            pl.BlockSpec(memory_space=pl.ANY),
        ],
        out_specs=(pl.BlockSpec(memory_space=pl.ANY), pl.BlockSpec(memory_space=pltpu.VMEM)),
        scratch_shapes=[
            pltpu.VMEM((RT * size, window), BF16),
            pltpu.VMEM((number, size, size), BF16),
            pltpu.VMEM((window, width), BF16),
            pltpu.VMEM((size, size), F32),
            pltpu.SMEM((places,), jnp.int32),
            pltpu.SMEM((places,), jnp.int32),
            pltpu.SMEM((number,), jnp.int32),
            pltpu.SemaphoreType.DMA((number,)),
            pltpu.SemaphoreType.DMA,
            pltpu.SemaphoreType.DMA((RT,)),
        ],
        compiler_params=pltpu.CompilerParams(vmem_limit_bytes=40 * 1024 * 1024),
    )(slots, count, tiles, feats)


def remote(src, dst, send_sem, recv_sem, device):
    return pltpu.make_async_remote_copy(
        src_ref=src, dst_ref=dst, send_sem=send_sem, recv_sem=recv_sem,
        device_id=device, device_id_type=MESH,
    )


def exchange_kernel(n_row, n_col, scale, block, partial, weight, out_grad,
                    activated, weight_grad, window_grad,
                    dense, core_in, pair_out, pair_in, grads, cross_out, cross_in,
                    chain_out, chain_in, total, ready, local, piece_in, piece, step_in, whole,
                    dense_sem, core_sem, pair_sem, own_sem, far_sem, pass_sem, cross_sem,
                    chain_sem, piece_sem, step_sem, whole_sem):
    n_z, n_y = n_row // 2, n_col // 2
    row, col = lax.axis_index("row"), lax.axis_index("col")
    z, x = row // 2, row % 2
    y, core = col // 2, col % 2
    share = out_grad.shape[0]
    span = window_grad.shape[0]
    width = weight.shape[0]
    depth = width // n_col
    steps = n_row.bit_length() - 1

    dense_copy = pltpu.make_async_copy(block, dense, dense_sem)
    dense_copy.start()

    sibling = (row, y * 2 + 1 - core)
    mirror = (z * 2 + 1 - x, col)
    col_peers = [(row, (col + d) % n_col) for d in range(1, n_col)]
    swaps = []
    for s in range(steps):
        bit = 1 << s
        swaps.append((row + bit - row // bit % 2 * 2 * bit, col))
    ring = [((row + 2) % n_row, col), ((row + n_row - 2) % n_row, col)]

    barrier = pltpu.get_barrier_semaphore()
    greeted = col_peers + swaps + ring
    for device in greeted:
        pl.semaphore_signal(barrier, inc=1, device_id=device, device_id_type=MESH)
    pl.semaphore_wait(barrier, len(greeted))

    started = []

    def send(copy):
        copy.start()
        started.append(copy)

    def rows_of(index, length):
        if isinstance(index, int):
            return pl.ds(index * length, length)
        return pl.ds(pl.multiple_of(index * length, length), length)

    core_copies = []
    for d in list(range(1, n_y)) + [0]:
        owner = (y + d) % n_y * 2 + 1 - core
        copy = remote(partial.at[rows_of(owner, share)], core_in.at[d],
                      core_sem.at[0, d], core_sem.at[1, d], sibling)
        send(copy)
        core_copies.append(copy)
    pair_copies = []
    for d in range(1, n_y):
        core_copies[d - 1].wait_recv()
        owner = (y + d) % n_y * 2 + core
        pair_out[d - 1] = (
            partial[rows_of(owner, share), :].astype(F32) + core_in[d].astype(F32)
        ).astype(BF16)
        copy = remote(pair_out.at[d - 1], pair_in.at[d - 1],
                      pair_sem.at[0, d - 1], pair_sem.at[1, d - 1], (row, owner))
        send(copy)
        pair_copies.append(copy)
    core_copies[-1].wait_recv()
    sums = partial[rows_of(col, share), :].astype(F32) + core_in[0].astype(F32)
    for d in range(1, n_y):
        pair_copies[d - 1].wait_recv()
        sums = sums + pair_in[d - 1].astype(F32)
    aggregated = sums.astype(BF16)

    pre_act = jnp.dot(aggregated, weight[...], preferred_element_type=F32)
    sigmoid_pre = jax.nn.sigmoid(pre_act)
    grad_pre = (
        out_grad[...].astype(F32) * sigmoid_pre * (1.0 + pre_act * (1.0 - sigmoid_pre))
    ).astype(BF16)
    grads[rows_of(col, share), :] = lax.dot_general(
        grad_pre, weight[...], (((1,), (1,)), ((), ())), preferred_element_type=F32
    ).astype(BF16)

    mine = grads.at[rows_of(col, share)]
    far_copies = []
    for d in range(1, n_y):
        copy = remote(mine, mine, far_sem.at[0, d - 1], far_sem.at[1, d - 1],
                      (row, (y + d) % n_y * 2 + core))
        send(copy)
        far_copies.append(copy)
    own_copy = remote(mine, mine, own_sem.at[0], own_sem.at[1], sibling)
    send(own_copy)

    activated[...] = (pre_act * sigmoid_pre).astype(BF16)
    local[...] = lax.dot_general(
        aggregated, grad_pre, (((0,), (0,)), ((), ())), preferred_element_type=F32
    )
    piece_copies = []
    for d in range(1, n_col):
        copy = remote(local.at[rows_of((col + d) % n_col, depth)], piece_in.at[d - 1],
                      piece_sem.at[0, d - 1], piece_sem.at[1, d - 1], col_peers[d - 1])
        send(copy)
        piece_copies.append(copy)

    pass_copies = []
    for d in range(1, n_y):
        far_copies[d - 1].wait_recv()
        got = grads.at[rows_of((y + n_y - d) % n_y * 2 + core, share)]
        copy = remote(got, got, pass_sem.at[0, d - 1], pass_sem.at[1, d - 1], sibling)
        send(copy)
        pass_copies.append(copy)
    own_copy.wait_recv()
    for copy in pass_copies:
        copy.wait_recv()
    dense_copy.wait()

    def columns_product(index, length):
        return lax.dot_general(
            dense[:, rows_of(index, length)], grads[...],
            (((0,), (0,)), ((), ())), preferred_element_type=F32,
        )

    narrow = span % LANES != 0
    if narrow:
        for tile in range(dense.shape[1] // width):
            ready[rows_of(tile, width), :] = columns_product(tile, width)

    def product(owner):
        if narrow:
            return ready[rows_of(owner, span), :]
        return columns_product(owner, span)

    high = (2 * z >= n_z).astype(jnp.int32)
    low_z = z + high * (n_z - 1 - 2 * z)

    def order(i):
        lead = n_z - 1 - 2 * low_z
        m = i - lead
        early = (m < 0).astype(jnp.int32)
        odd = jnp.abs(m) % 2
        late = (1 - odd) * (m // 2) + odd * (2 * low_z - m // 2)
        at = early * (n_z - 1 - i) + (1 - early) * late
        return at + high * (n_z - 1 - 2 * at)

    def cross_copy(at):
        return remote(cross_out.at[at], cross_in.at[at],
                      cross_sem.at[0, at], cross_sem.at[1, at], mirror)

    for i in range(n_z):
        at = order(i)
        cross_out[at] = product(at * 2 + 1 - x).astype(BF16)
        send(cross_copy(at))

    def swap_copy(s):
        return remote(piece.at[s], step_in.at[s], step_sem.at[0, s], step_sem.at[1, s], swaps[s])

    swap_copies, whole_copies = [], []

    def next_swap(s):
        if s == 0:
            added = local[rows_of(col, depth), :]
            for copy in piece_copies:
                copy.wait_recv()
            for d in range(1, n_col):
                added = added + piece_in[d - 1]
        elif s <= steps:
            swap_copies[s - 1].wait_recv()
            added = piece[s - 1] + step_in[s - 1]
        if s < steps:
            piece[s] = added
            copy = swap_copy(s)
            send(copy)
            swap_copies.append(copy)
        elif s == steps:
            spot = whole.at[rows_of(col, depth)]
            spot[...] = added * scale
            for d in range(1, n_col):
                copy = remote(spot, spot, whole_sem.at[0, d - 1], whole_sem.at[1, d - 1],
                              col_peers[d - 1])
                send(copy)
                whole_copies.append(copy)

    def chain_copy(at):
        up = (at > z).astype(jnp.int32)
        return remote(chain_out.at[at], chain_in.at[up, at],
                      chain_sem.at[0, up, at], chain_sem.at[1, up, at],
                      (row + 4 * up - 2, col))

    def await_chain(up, at):
        remote(chain_out.at[at], chain_in.at[up, at], chain_sem.at[0, up, at],
               chain_sem.at[1, up, at], mirror).wait_recv()
        total[...] += chain_in[up, at].astype(F32)

    next_swap(0)
    for i in range(n_z):
        at = order(i)
        total[...] = product(at * 2 + x)
        cross_copy(at).wait_recv()
        total[...] += cross_in[at].astype(F32)

        @pl.when(jnp.logical_and(z > 0, at >= z))
        def _():
            await_chain(1, at)

        @pl.when(jnp.logical_and(z < n_z - 1, at <= z))
        def _():
            await_chain(0, at)

        if i < n_z - 1:
            chain_out[at] = total[...].astype(BF16)
            chain_copy(at).start()
        else:
            window_grad[...] = total[...].astype(BF16)
        next_swap(i + 1)
    for s in range(n_z + 1, steps + 1):
        next_swap(s)
    for copy in whole_copies:
        copy.wait_recv()
    weight_grad[...] = whole[...]
    for copy in started:
        copy.wait_send()
    for i in range(n_z - 1):
        chain_copy(order(i)).wait_send()


def exchange(n_row, n_col, block, partial, weight, out_grad):
    rows, window = block.shape
    width = weight.shape[0]
    share = out_grad.shape[0]
    span = window // n_row
    n_z, n_y = n_row // 2, n_col // 2
    depth = width // n_col
    steps = n_row.bit_length() - 1
    dma = pltpu.SemaphoreType.DMA
    vmem = pl.BlockSpec(memory_space=pltpu.VMEM)
    return pl.pallas_call(
        functools.partial(exchange_kernel, n_row, n_col, 1.0 / math.sqrt(rows * n_row)),
        out_shape=(
            jax.ShapeDtypeStruct((share, width), BF16),
            jax.ShapeDtypeStruct((width, width), F32),
            jax.ShapeDtypeStruct((span, width), BF16),
        ),
        in_specs=[pl.BlockSpec(memory_space=pl.ANY), vmem, vmem, vmem],
        out_specs=(vmem, vmem, vmem),
        scratch_shapes=[
            pltpu.VMEM((rows, window), BF16),
            pltpu.VMEM((n_y, share, width), BF16),
            pltpu.VMEM((n_y - 1, share, width), BF16),
            pltpu.VMEM((n_y - 1, share, width), BF16),
            pltpu.VMEM((rows, width), BF16),
            pltpu.VMEM((n_z, span, width), BF16),
            pltpu.VMEM((n_z, span, width), BF16),
            pltpu.VMEM((n_z, span, width), BF16),
            pltpu.VMEM((2, n_z, span, width), BF16),
            pltpu.VMEM((span, width), F32),
            pltpu.VMEM((window if span % LANES else 8, width), F32),
            pltpu.VMEM((width, width), F32),
            pltpu.VMEM((n_col - 1, depth, width), F32),
            pltpu.VMEM((steps, depth, width), F32),
            pltpu.VMEM((steps, depth, width), F32),
            pltpu.VMEM((width, width), F32),
            dma,
            dma((2, n_y)),
            dma((2, n_y - 1)),
            dma((2,)),
            dma((2, n_y - 1)),
            dma((2, n_y - 1)),
            dma((2, n_z)),
            dma((2, 2, n_z)),
            dma((2, n_col - 1)),
            dma((2, steps)),
            dma((2, n_col - 1)),
        ],
        compiler_params=pltpu.CompilerParams(
            collective_id=0, has_side_effects=True, vmem_limit_bytes=40 * 1024 * 1024
        ),
    )(block, partial, weight, out_grad)


def on_device(n_row, n_col, tiles, tile_slot, tile_count, feats, weight, out_grad):
    block, partial = block_product(tiles[0], tile_slot[0], tile_count[0], feats)
    activated, weight_grad, window_grad = exchange(
        n_row, n_col, block, partial, weight, out_grad
    )
    return activated, weight_grad, window_grad[None]


def solution(mesh):
    placed = (
        P("row", "col", None, None),
        P("row", "col"),
        P("row", "col"),
        P("col", None),
        P(),
        P(("row", "col"), None),
    )
    return jax.shard_map(
        functools.partial(on_device, mesh.shape["row"], mesh.shape["col"]),
        mesh=mesh,
        in_specs=placed,
        out_specs=(P(("row", "col"), None), P(), P("col", "row", None)),
        check_vma=False,
    )
```

time: 461 us -> 59.4 us (0.13); the launches traced: 456 us -> 59.1 us
  waiting for transfers between devices: 328 us -> 0 us
  loops' own time: 64.5 us -> 0 us
  Pallas kernels: 0 us -> 52 us
  matrix products: 19.2 us -> 0 us
  local copies, waits for them, and re-layouts: 20.1 us -> 5.78 us
  between operations: 13.8 us -> 1.32 us
  blocking collectives: 6.78 us -> 0 us
    reduce_scatter x2 -> x0, waiting for transfers between devices: 256 us -> none  [the longest x1 144 us: on_device(): lax.psum_scatter(row_partial, 'col', scatter_dimension=0, tiled=True)]
    psum x1 -> x0, waiting for transfers between devices: 71.7 us -> none  [on_device(): weight_grad = lax.psum(local_grad, ('row', 'col')) * grad_scale]
    another operation x2 -> x0, loops' own time: 64.5 us -> none  [tile_products(): return lax.fori_loop(0, live_count, one_step, initial)]
    pallas_call x0 -> x2, Pallas kernels: none -> 52 us  [the longest x1 44.1 us: exchange(): pl.pallas_call(functools.partial(exchange_kernel, n_row, n_col, 1.0 / mat...]
    dot_general x17 -> x0, matrix products: 19.2 us -> none  [the longest x7 8.13 us: one_step(): jnp.dot(one_block, source_block, preferred_element_type=jnp.float32)]
    dynamic_slice x42 -> x0, local copies, waits for them, and re-layouts: 17.5 us -> none  [the longest x14 8.6 us: one_step(): take_index[position]]
    all_gather x1 -> x0, blocking collectives: 6.78 us -> none  [on_device(): grad_block = lax.all_gather(grad_share, 'col', axis=0, tiled=True)]
  transfers between devices with their start and end apart: 3 -> 0, of which waited for: 3 -> 0; matrix products, arithmetic and copies ran while one was open for 4% -> 0% of each run, Pallas kernels for 0% -> 0%
where the time goes in v1:
time: 59.4 us; the launch traced here: 59.1 us
  Pallas kernels  52 us (88%)
  local copies, waits for them, and re-layouts  5.78 us (10%)
  between operations  1.32 us (2%)
    pallas_call x1, Pallas kernels, exchange(): pl.pallas_call(functools.partial(exchange_kernel, n_row, n_col, 1.0 / mat...  44.1 us
    pallas_call x1, Pallas kernels, block_product(): pl.pallas_call(block_kernel, out_shape=(jax.ShapeDtypeStruct((RT * size,...  7.91 us
    unnamed x13, local copies, waits for them, and re-layouts  5.78 us

profile of v1, /device:TPU:0, one launch (start us, length us, event | category | flops | bytes accessed | tf_op | source)
XLA Modules:
  0.0 59.1 jit_solution(4707947063851356654)
XLA Ops:
  1.3 0.0 copy-start
  1.3 1.9 %copy-done = bf16[1,24,256,256]{3,2,1,0:T(8,128)(2,1)S(1)} copy-done((bf16[1,24,256,256]{3,2,1,0:T(8,128)(2,1)S(1)}, bf16[1,24,256,256]{3,2,1,0:T(8,128)(2,1)}, u32[]{:S(2)}) %copy-start) | copy-done | bytes 3145752
  3.2 0.0 copy-start.1
  3.2 1.2 %copy-done.1 = bf16[2048,256]{1,0:T(8,128)(2,1)S(1)} copy-done((bf16[2048,256]{1,0:T(8,128)(2,1)S(1)}, bf16[2048,256]{1,0:T(8,128)(2,1)}, u32[]{:S(2)}) %copy-start.1) | copy-done | bytes 1048600
  4.4 0.0 copy-start.4
  4.4 0.7 %copy-done.4 = s32[1,24]{1,0:T(1,128)S(1)} copy-done((s32[1,24]{1,0:T(1,128)S(1)}, s32[1,24]{1,0:T(1,128)}, u32[]{:S(2)}) %copy-start.4) | copy-done | bytes 120
  5.0 0.0 copy-start.2
  5.1 0.0 copy-start.3
  5.1 7.9 %shard_map.85 = (bf16[1024,2048]{1,0:T(8,128)(2,1)S(1)}, bf16[1024,256]{1,0:T(8,128)(2,1)S(1)}) custom-call(s32[24]{0:T(128)S(1)} %bitcast.7, s32[1]{0:T(128)} %bitcast.4.count, bf16[24,256,256]{2,1,0:T(8,128)(2,1)S(1)} %bitcast.5, bf16[2048,256]{1,0:T(8,128)(2,1)S(1)} %copy-done.1), custom_call_target="tpu_custom_call" | custom-call | tf_op jit(solution)/shard_map/pallas_call | solution.py:104
  13.0 0.0 copy-done.2
  13.0 0.0 copy-done.3
  13.0 44.1 %shard_map.86 = (bf16[256,256]{1,0:T(8,128)(2,1)S(1)}, f32[256,256]{1,0:T(8,128)S(1)}, bf16[256,256]{1,0:T(8,128)(2,1)S(1)}) custom-call(bf16[1024,2048]{1,0:T(8,128)(2,1)S(1)} %get-tuple-element.8.block, bf16[1024,256]{1,0:T(8,128)(2,1)S(1)} %get-tuple-element.9.partial, bf16[256,256]{1,0:T(8,128)(2,1)S(1)} %copy-done.2, bf16[256,256]{1,0:T(8,128)(2,1)S(1)} %copy-done.3), custom_call_target="tpu_custom_call" | custom-call | tf_op jit(solution)/shard_map/pallas_call | solution.py:371
  57.1 0.7 %copy.13 = bf16[256,256]{1,0:T(8,128)(2,1)} copy(bf16[256,256]{1,0:T(8,128)(2,1)S(1)} %get-tuple-element.16) | data formatting | bytes 262144
  57.7 0.7 %copy.14 = f32[256,256]{1,0:T(8,128)} copy(f32[256,256]{1,0:T(8,128)S(1)} %get-tuple-element.17) | data formatting | bytes 524288
  58.4 0.7 %copy.15 = bf16[1,256,256]{2,1,0:T(8,128)(2,1)} copy(bf16[1,256,256]{2,1,0:T(8,128)(2,1)S(1)} %bitcast.6) | data formatting | bytes 262144
Async XLA Ops:
  1.3 1.9 %copy-start = (bf16[1,24,256,256]{3,2,1,0:T(8,128)(2,1)S(1)}, bf16[1,24,256,256]{3,2,1,0:T(8,128)(2,1)}, u32[]{:S(2)}) copy-start(bf16[1,24,256,256]{3,2,1,0:T(8,128)(2,1)} %param.6) | copy-start | bytes 9437188
  3.2 1.2 %copy-start.1 = (bf16[2048,256]{1,0:T(8,128)(2,1)S(1)}, bf16[2048,256]{1,0:T(8,128)(2,1)}, u32[]{:S(2)}) copy-start(bf16[2048,256]{1,0:T(8,128)(2,1)} %feats.1) | copy-start | bytes 3145732
  4.4 0.7 %copy-start.4 = (s32[1,24]{1,0:T(1,128)S(1)}, s32[1,24]{1,0:T(1,128)}, u32[]{:S(2)}) copy-start(s32[1,24]{1,0:T(1,128)} %param.7) | copy-start | bytes 292
  5.0 7.9 %copy-start.2 = (bf16[256,256]{1,0:T(8,128)(2,1)S(1)}, bf16[256,256]{1,0:T(8,128)(2,1)}, u32[]{:S(2)}) copy-start(bf16[256,256]{1,0:T(8,128)(2,1)} %weight.1) | copy-start | bytes 393220
  5.1 7.9 %copy-start.3 = (bf16[256,256]{1,0:T(8,128)(2,1)S(1)}, bf16[256,256]{1,0:T(8,128)(2,1)}, u32[]{:S(2)}) copy-start(bf16[256,256]{1,0:T(8,128)(2,1)} %out_grad.1) | copy-start | bytes 393220

commit v2 on v1

v2 whole, which is shorter than its diff:
```python
import functools
import math

import jax
import jax.numpy as jnp
from jax import lax
from jax.experimental import pallas as pl
from jax.experimental.pallas import tpu as pltpu
from jax.sharding import PartitionSpec as P

RT = 4
LANES = 128
PARTS = 2
MESH = pl.DeviceIdType.MESH
F32 = jnp.float32
BF16 = jnp.bfloat16


def block_kernel(slot_list, live_count, tiles, feats, block, partial, extra, source, total,
                 slots, count, first, others, following, list_sem, tile_sem, feat_sem):
    size = tiles.shape[1]
    col_tiles = feats.shape[0] // size
    places = RT * col_tiles

    list_copies = [
        pltpu.make_async_copy(slot_list, slots, list_sem.at[0]),
        pltpu.make_async_copy(live_count, count, list_sem.at[1]),
    ]
    for copy in list_copies:
        copy.start()
    feat_copy = pltpu.make_async_copy(feats, source, feat_sem)
    feat_copy.start()

    def place_of(slot):
        row = pl.multiple_of(slot // col_tiles * size, size)
        column = pl.multiple_of(slot % col_tiles * size, size)
        return block.at[pl.ds(row, size), pl.ds(column, size)]

    for place in range(places):
        first[place] = -1
        others[place] = -1
    for copy in list_copies:
        copy.wait()
    live = count[0, 0]

    @pl.loop(0, live)
    def _(position):
        slot = slots[0, position]
        taken = first[slot] >= 0

        @pl.when(jnp.logical_not(taken))
        def _():
            first[slot] = position
            pltpu.make_async_copy(tiles.at[position], place_of(slot), tile_sem.at[position]).start()

        @pl.when(taken)
        def _():
            following[position] = others[slot]
            others[slot] = position
            pltpu.make_async_copy(
                tiles.at[position], extra.at[position], tile_sem.at[position]
            ).start()

    @pl.loop(0, places)
    def _(place):
        @pl.when(first[place] < 0)
        def _():
            place_of(place)[...] = jnp.zeros((size, size), BF16)

    def await_tile(position):
        pltpu.make_async_copy(
            tiles.at[position], extra.at[position], tile_sem.at[position]
        ).wait()

    for row in range(RT):
        @pl.loop(row * col_tiles, (row + 1) * col_tiles)
        def _(place):
            @pl.when(first[place] >= 0)
            def _():
                await_tile(first[place])

                @pl.when(others[place] >= 0)
                def _():
                    spot = place_of(place)
                    total[...] = spot[...].astype(F32)

                    def add(position):
                        await_tile(position)
                        total[...] += extra[position].astype(F32)
                        return following[position]

                    lax.while_loop(lambda position: position >= 0, add, others[place])
                    spot[...] = total[...].astype(BF16)

        rows = pl.ds(row * size, size)
        if row == 0:
            feat_copy.wait()
        partial[rows, :] = jnp.dot(
            block[rows, :], source[...], preferred_element_type=F32
        ).astype(BF16)


def block_product(tiles, slots, count, feats):
    number, size, _ = tiles.shape
    window, width = feats.shape
    places = RT * window // size
    hbm = pl.BlockSpec(memory_space=pltpu.HBM)
    vmem = pl.BlockSpec(memory_space=pltpu.VMEM)
    return pl.pallas_call(
        block_kernel,
        out_shape=(
            jax.ShapeDtypeStruct((RT * size, window), BF16),
            jax.ShapeDtypeStruct((RT * size, width), BF16),
        ),
        in_specs=[hbm, hbm, hbm, hbm],
        out_specs=(vmem, vmem),
        scratch_shapes=[
            pltpu.VMEM((number, size, size), BF16),
            pltpu.VMEM((window, width), BF16),
            pltpu.VMEM((size, size), F32),
            pltpu.SMEM(slots.shape, jnp.int32),
            pltpu.SMEM(count.shape, jnp.int32),
            pltpu.SMEM((places,), jnp.int32),
            pltpu.SMEM((places,), jnp.int32),
            pltpu.SMEM((number,), jnp.int32),
            pltpu.SemaphoreType.DMA((2,)),
            pltpu.SemaphoreType.DMA((number,)),
            pltpu.SemaphoreType.DMA,
        ],
        compiler_params=pltpu.CompilerParams(vmem_limit_bytes=24 * 1024 * 1024),
    )(slots, count, tiles, feats)


def publish_kernel(*refs):
    number = len(refs) // 2
    sem = refs[-1]
    copies = [
        pltpu.make_async_copy(refs[i], refs[number + i], sem.at[i]) for i in range(number)
    ]
    for copy in copies:
        copy.start()
    for copy in copies:
        copy.wait()


def publish(*results):
    return pl.pallas_call(
        publish_kernel,
        out_shape=tuple(jax.ShapeDtypeStruct(r.shape, r.dtype) for r in results),
        in_specs=[pl.BlockSpec(memory_space=pltpu.VMEM)] * len(results),
        out_specs=tuple(pl.BlockSpec(memory_space=pltpu.HBM) for _ in results),
        scratch_shapes=[pltpu.SemaphoreType.DMA((len(results),))],
    )(*results)


def remote(src, dst, send_sem, recv_sem, device):
    return pltpu.make_async_remote_copy(
        src_ref=src, dst_ref=dst, send_sem=send_sem, recv_sem=recv_sem,
        device_id=device, device_id_type=MESH,
    )


def exchange_kernel(n_row, n_col, scale, block, partial, weight, out_grad,
                    activated, weight_grad, window_grad,
                    core_in, pair_out, pair_in, grads, grads_wide, cross_out, cross_in,
                    chain_out, chain_in, total, ready, local, piece_in, piece, step_in, whole,
                    core_sem, pair_sem, own_sem, far_sem, pass_sem, cross_sem,
                    chain_sem, piece_sem, step_sem, whole_sem):
    n_z, n_y = n_row // 2, n_col // 2
    row, col = lax.axis_index("row"), lax.axis_index("col")
    z, x = row // 2, row % 2
    y, core = col // 2, col % 2
    share = out_grad.shape[0]
    span = window_grad.shape[0]
    width = weight.shape[0]
    depth = width // n_col
    steps = n_row.bit_length() - 1
    cut = share // PARTS

    sibling = (row, y * 2 + 1 - core)
    mirror = (z * 2 + 1 - x, col)
    col_peers = [(row, (col + d) % n_col) for d in range(1, n_col)]
    swaps = []
    for s in list(range(1, steps)) + [0]:
        bit = 1 << s
        swaps.append((row + bit - row // bit % 2 * 2 * bit, col))
    ring = [((row + 2) % n_row, col), ((row + n_row - 2) % n_row, col)]

    barrier = pltpu.get_barrier_semaphore()
    greeted = col_peers + swaps + ring
    for device in greeted:
        pl.semaphore_signal(barrier, inc=1, device_id=device, device_id_type=MESH)
    pl.semaphore_wait(barrier, len(greeted))

    started = []

    def send(*args):
        copy = remote(*args)
        copy.start()
        started.append(copy)
        return copy

    def rows_of(index, length):
        if isinstance(index, int):
            return pl.ds(index * length, length)
        return pl.ds(pl.multiple_of(index * length, length), length)

    def part_of(owner, part):
        return rows_of(owner * PARTS + part, cut)

    core_copies = {}
    for d in list(range(1, n_y)) + [0]:
        for part in range(PARTS):
            owner = (y + d) % n_y * 2 + 1 - core
            core_copies[d, part] = send(
                partial.at[part_of(owner, part)], core_in.at[d, part],
                core_sem.at[0, d, part], core_sem.at[1, d, part], sibling)
    pair_copies = {}
    for part in range(PARTS):
        for d in range(1, n_y):
            core_copies[d, part].wait_recv()
            owner = (y + d) % n_y * 2 + core
            pair_out[d - 1, part] = (
                partial[part_of(owner, part), :].astype(F32) + core_in[d, part].astype(F32)
            ).astype(BF16)
            pair_copies[d, part] = send(
                pair_out.at[d - 1, part], pair_in.at[d - 1, part],
                pair_sem.at[0, d - 1, part], pair_sem.at[1, d - 1, part], (row, owner))

    far_copies, own_copies = {}, []
    for part in range(PARTS):
        core_copies[0, part].wait_recv()
        sums = partial[part_of(col, part), :].astype(F32) + core_in[0, part].astype(F32)
        for d in range(1, n_y):
            pair_copies[d, part].wait_recv()
            sums = sums + pair_in[d - 1, part].astype(F32)
        aggregated = sums.astype(BF16)
        pre_act = jnp.dot(aggregated, weight[...], preferred_element_type=F32)
        sigmoid_pre = jax.nn.sigmoid(pre_act)
        rows = pl.ds(part * cut, cut)
        grad_pre = (
            out_grad[rows, :].astype(F32) * sigmoid_pre * (1.0 + pre_act * (1.0 - sigmoid_pre))
        ).astype(BF16)
        grads[col, part] = lax.dot_general(
            weight[...], grad_pre, (((1,), (1,)), ((), ())), preferred_element_type=F32
        ).astype(BF16)
        mine = grads.at[col, part]
        for d in range(1, n_y):
            far_copies[d, part] = send(
                mine, mine, far_sem.at[0, d - 1, part], far_sem.at[1, d - 1, part],
                (row, (y + d) % n_y * 2 + core))
        own_copies.append(send(mine, mine, own_sem.at[0, part], own_sem.at[1, part], sibling))
        activated[rows, :] = (pre_act * sigmoid_pre).astype(BF16)
        outer = lax.dot_general(
            aggregated, grad_pre, (((0,), (0,)), ((), ())), preferred_element_type=F32
        )
        if part == 0:
            local[...] = outer
        else:
            local[...] += outer

    piece_copies = []
    for d in range(1, n_col):
        piece_copies.append(send(
            local.at[rows_of((col + d) % n_col, depth)], piece_in.at[d - 1],
            piece_sem.at[0, d - 1], piece_sem.at[1, d - 1], col_peers[d - 1]))

    pass_copies = []
    for part in range(PARTS):
        for d in range(1, n_y):
            far_copies[d, part].wait_recv()
            got = grads.at[(y + n_y - d) % n_y * 2 + core, part]
            pass_copies.append(send(
                got, got, pass_sem.at[0, d - 1, part], pass_sem.at[1, d - 1, part], sibling))
    for copy in own_copies + pass_copies:
        copy.wait_recv()
    for owner in range(n_col):
        for part in range(PARTS):
            grads_wide[:, part_of(owner, part)] = grads[owner, part]

    def columns_product(index, length):
        return jnp.dot(
            grads_wide[...], block[:, rows_of(index, length)], preferred_element_type=F32
        )

    narrow = span % LANES != 0
    if narrow:
        for tile in range(block.shape[1] // width):
            ready[rows_of(tile, width), :] = columns_product(tile, width).T

    def product(owner):
        if narrow:
            return ready[rows_of(owner, span), :]
        return columns_product(owner, span)

    high = (2 * z >= n_z).astype(jnp.int32)
    low_z = z + high * (n_z - 1 - 2 * z)

    def order(i):
        lead = n_z - 1 - 2 * low_z
        m = i - lead
        early = (m < 0).astype(jnp.int32)
        odd = jnp.abs(m) % 2
        late = (1 - odd) * (m // 2) + odd * (2 * low_z - m // 2)
        at = early * (n_z - 1 - i) + (1 - early) * late
        return at + high * (n_z - 1 - 2 * at)

    slab = total.shape[0] // PARTS

    def cross_copy(at, part):
        rows = pl.ds(part * slab, slab)
        return (cross_out.at[at, rows], cross_in.at[at, rows],
                cross_sem.at[0, at, part], cross_sem.at[1, at, part], mirror)

    for i in range(n_z):
        at = order(i)
        cross_out[at] = product(at * 2 + 1 - x).astype(BF16)
        for part in range(PARTS):
            send(*cross_copy(at, part))

    swap_copies, whole_copies = [], []

    def next_swap(s):
        if s == 0:
            added = local[rows_of(col, depth), :]
            for copy in piece_copies:
                copy.wait_recv()
            for d in range(1, n_col):
                added = added + piece_in[d - 1]
        elif s <= steps:
            swap_copies[s - 1].wait_recv()
            added = piece[s - 1] + step_in[s - 1]
        if s < steps:
            piece[s] = added
            swap_copies.append(send(
                piece.at[s], step_in.at[s], step_sem.at[0, s], step_sem.at[1, s], swaps[s]))
        elif s == steps:
            spot = whole.at[rows_of(col, depth)]
            spot[...] = added * scale
            for d in range(1, n_col):
                whole_copies.append(send(
                    spot, spot, whole_sem.at[0, d - 1], whole_sem.at[1, d - 1],
                    col_peers[d - 1]))

    def chain_copy(at, part):
        rows = pl.ds(part * slab, slab)
        up = (at > z).astype(jnp.int32)
        return remote(chain_out.at[at, rows], chain_in.at[up, at, rows],
                      chain_sem.at[0, up, at, part], chain_sem.at[1, up, at, part],
                      (row + 4 * up - 2, col))

    def await_chain(up, at, part):
        rows = pl.ds(part * slab, slab)
        remote(chain_out.at[at, rows], chain_in.at[up, at, rows],
               chain_sem.at[0, up, at, part], chain_sem.at[1, up, at, part], mirror).wait_recv()
        total[rows, :] += chain_in[up, at, rows, :].astype(F32)

    next_swap(0)
    for i in range(n_z):
        at = order(i)
        total[...] = product(at * 2 + x)
        for part in range(PARTS):
            rows = pl.ds(part * slab, slab)
            remote(*cross_copy(at, part)).wait_recv()
            total[rows, :] += cross_in[at, rows, :].astype(F32)

            @pl.when(jnp.logical_and(z > 0, at >= z))
            def _():
                await_chain(1, at, part)

            @pl.when(jnp.logical_and(z < n_z - 1, at <= z))
            def _():
                await_chain(0, at, part)

            if i < n_z - 1:
                chain_out[at, rows, :] = total[rows, :].astype(BF16)
                chain_copy(at, part).start()
        if i == n_z - 1:
            result = total[...] if narrow else total[...].T
            window_grad[...] = result.astype(BF16)
        next_swap(i + 1)
    for s in range(n_z + 1, steps + 1):
        next_swap(s)
    for copy in whole_copies:
        copy.wait_recv()
    weight_grad[...] = whole[...]
    for copy in started:
        copy.wait_send()
    for i in range(n_z - 1):
        for part in range(PARTS):
            chain_copy(order(i), part).wait_send()


def exchange(n_row, n_col, block, partial, weight, out_grad):
    rows, window = block.shape
    width = weight.shape[0]
    share = out_grad.shape[0]
    span = window // n_row
    n_z, n_y = n_row // 2, n_col // 2
    depth = width // n_col
    steps = n_row.bit_length() - 1
    cut = share // PARTS
    narrow = span % LANES != 0
    chunk = (span, width) if narrow else (width, span)
    dma = pltpu.SemaphoreType.DMA
    vmem = pl.BlockSpec(memory_space=pltpu.VMEM)
    return pl.pallas_call(
        functools.partial(exchange_kernel, n_row, n_col, 1.0 / math.sqrt(rows * n_row)),
        out_shape=(
            jax.ShapeDtypeStruct((share, width), BF16),
            jax.ShapeDtypeStruct((width, width), F32),
            jax.ShapeDtypeStruct((span, width), BF16),
        ),
        in_specs=[vmem, vmem, vmem, vmem],
        out_specs=(vmem, vmem, vmem),
        scratch_shapes=[
            pltpu.VMEM((n_y, PARTS, cut, width), BF16),
            pltpu.VMEM((n_y - 1, PARTS, cut, width), BF16),
            pltpu.VMEM((n_y - 1, PARTS, cut, width), BF16),
            pltpu.VMEM((n_col, PARTS, width, cut), BF16),
            pltpu.VMEM((width, rows), BF16),
            pltpu.VMEM((n_z, *chunk), BF16),
            pltpu.VMEM((n_z, *chunk), BF16),
            pltpu.VMEM((n_z, *chunk), BF16),
            pltpu.VMEM((2, n_z, *chunk), BF16),
            pltpu.VMEM(chunk, F32),
            pltpu.VMEM((window if narrow else 8, width), F32),
            pltpu.VMEM((width, width), F32),
            pltpu.VMEM((n_col - 1, depth, width), F32),
            pltpu.VMEM((steps, depth, width), F32),
            pltpu.VMEM((steps, depth, width), F32),
            pltpu.VMEM((width, width), F32),
            dma((2, n_y, PARTS)),
            dma((2, n_y - 1, PARTS)),
            dma((2, PARTS)),
            dma((2, n_y - 1, PARTS)),
            dma((2, n_y - 1, PARTS)),
            dma((2, n_z, PARTS)),
            dma((2, 2, n_z, PARTS)),
            dma((2, n_col - 1)),
            dma((2, steps)),
            dma((2, n_col - 1)),
        ],
        compiler_params=pltpu.CompilerParams(
            collective_id=0, has_side_effects=True, vmem_limit_bytes=40 * 1024 * 1024
        ),
    )(block, partial, weight, out_grad)


def on_device(n_row, n_col, tiles, tile_slot, tile_count, feats, weight, out_grad):
    held = [
        pltpu.with_memory_space_constraint(array, pltpu.HBM)
        for array in (tiles[0], tile_slot, feats)
    ]
    block, partial = block_product(held[0], held[1], tile_count, held[2])
    activated, weight_grad, window_grad = exchange(
        n_row, n_col, block, partial, weight, out_grad
    )
    activated, weight_grad, window_grad = publish(activated, weight_grad, window_grad)
    return activated, weight_grad, window_grad[None]


def solution(mesh):
    placed = (
        P("row", "col", None, None),
        P("row", "col"),
        P("row", "col"),
        P("col", None),
        P(),
        P(("row", "col"), None),
    )
    return jax.shard_map(
        functools.partial(on_device, mesh.shape["row"], mesh.shape["col"]),
        mesh=mesh,
        in_specs=placed,
        out_specs=(P(("row", "col"), None), P(), P("col", "row", None)),
        check_vma=False,
    )
```

time: 59.4 us -> 49.5 us (0.83)
  Pallas kernels: 52 us -> 46 us
  local copies, waits for them, and re-layouts: 5.78 us -> 2 us
    pallas_call x1, Pallas kernels: 44.1 us -> 39 us  [exchange(): pl.pallas_call(functools.partial(exchange_kernel, n_row, n_col, 1.0 / mat...]
    unnamed x13 -> x10, local copies, waits for them, and re-layouts: 5.78 us -> 2 us
    pallas_call x1, Pallas kernels: 7.91 us -> 5.14 us  [block_product(): pl.pallas_call(block_kernel, out_shape=(jax.ShapeDtypeStruct((RT * size,...]
    pallas_call x0 -> x1, Pallas kernels: none -> 1.85 us  [publish(): pl.pallas_call(publish_kernel, out_shape=tuple((jax.ShapeDtypeStruct(r.sh...]
where the time goes in v2:
time: 49.5 us; the launch traced here: 49.3 us
  Pallas kernels  46 us (93%)
  local copies, waits for them, and re-layouts  2 us (4%)
  between operations  1.38 us (3%)
    pallas_call x1, Pallas kernels, exchange(): pl.pallas_call(functools.partial(exchange_kernel, n_row, n_col, 1.0 / mat...  39 us
    pallas_call x1, Pallas kernels, block_product(): pl.pallas_call(block_kernel, out_shape=(jax.ShapeDtypeStruct((RT * size,...  5.14 us
    unnamed x10, local copies, waits for them, and re-layouts  2 us
    pallas_call x1, Pallas kernels, publish(): pl.pallas_call(publish_kernel, out_shape=tuple((jax.ShapeDtypeStruct(r.sh...  1.85 us

profile of v2, /device:TPU:0, one launch (start us, length us, event | category | flops | bytes accessed | tf_op | source)
XLA Modules:
  0.0 49.3 jit_solution(9626408855217695770)
XLA Ops:
  0.6 0.0 copy-start.2
  0.6 0.0 copy-start.1
  1.3 5.1 %shard_map.85 = (bf16[1024,2048]{1,0:T(8,128)(2,1)S(1)}, bf16[1024,256]{1,0:T(8,128)(2,1)S(1)}) custom-call(s32[1,24]{1,0:T(1,128)} %slot_list.1, s32[1,1]{1,0:T(1,128)S(6)} %copy.9.live_count, bf16[24,256,256]{2,1,0:T(8,128)(2,1)} %bitcast.2, bf16[2048,256]{1,0:T(8,128)(2,1)} %feats.1), custom_call_target="tpu_custom_call" | custom-call | tf_op jit(solution)/shard_map/pallas_call | solution.py:109
  6.5 0.0 copy-done.2
  6.5 0.0 copy-done.1
  6.5 39.0 %shard_map.86 = (bf16[256,256]{1,0:T(8,128)(2,1)S(1)}, f32[256,256]{1,0:T(8,128)S(1)}, bf16[256,256]{1,0:T(8,128)(2,1)S(1)}) custom-call(bf16[1024,2048]{1,0:T(8,128)(2,1)S(1)} %get-tuple-element.11.block, bf16[1024,256]{1,0:T(8,128)(2,1)S(1)} %get-tuple-element.12.partial, bf16[256,256]{1,0:T(8,128)(2,1)S(1)} %copy-done.1, bf16[256,256]{1,0:T(8,128)(2,1)S(1)} %copy-done.2), custom_call_target="tpu_custom_call" | custom-call | tf_op jit(solution)/shard_map/pallas_call | solution.py:407
  45.5 0.0 copy-start
  45.5 0.7 %copy-done = f32[256,256]{1,0:T(8,128)} copy-done((f32[256,256]{1,0:T(8,128)}, f32[256,256]{1,0:T(8,128)S(1)}, u32[]{:S(2)}) %copy-start) | copy-done | bytes 262168
  46.2 0.0 copy-start.3
  46.2 0.6 %copy-done.3 = bf16[256,256]{1,0:T(8,128)(2,1)} copy-done((bf16[256,256]{1,0:T(8,128)(2,1)}, bf16[256,256]{1,0:T(8,128)(2,1)S(1)}, u32[]{:S(2)}) %copy-start.3) | copy-done | bytes 131096
  46.8 0.0 copy-start.4
  46.8 0.6 %copy-done.4 = bf16[256,256]{1,0:T(8,128)(2,1)} copy-done((bf16[256,256]{1,0:T(8,128)(2,1)}, bf16[256,256]{1,0:T(8,128)(2,1)S(1)}, u32[]{:S(2)}) %copy-start.4) | copy-done | bytes 131096
  47.5 1.9 %shard_map.87 = (bf16[256,256]{1,0:T(8,128)(2,1)}, f32[256,256]{1,0:T(8,128)}, bf16[256,256]{1,0:T(8,128)(2,1)}) custom-call(bf16[256,256]{1,0:T(8,128)(2,1)} %copy-done.3, f32[256,256]{1,0:T(8,128)} %copy-done, bf16[256,256]{1,0:T(8,128)(2,1)} %copy-done.4), custom_call_target="tpu_custom_call" | custom-call | tf_op jit(solution)/shard_map/pallas_call | solution.py:147
Async XLA Ops:
  0.6 5.9 %copy-start.2 = (bf16[256,256]{1,0:T(8,128)(2,1)S(1)}, bf16[256,256]{1,0:T(8,128)(2,1)}, u32[]{:S(2)}) copy-start(bf16[256,256]{1,0:T(8,128)(2,1)} %out_grad.1) | copy-start | bytes 393220
  0.6 5.9 %copy-start.1 = (bf16[256,256]{1,0:T(8,128)(2,1)S(1)}, bf16[256,256]{1,0:T(8,128)(2,1)}, u32[]{:S(2)}) copy-start(bf16[256,256]{1,0:T(8,128)(2,1)} %weight.1) | copy-start | bytes 393220
  45.5 0.7 %copy-start = (f32[256,256]{1,0:T(8,128)}, f32[256,256]{1,0:T(8,128)S(1)}, u32[]{:S(2)}) copy-start(f32[256,256]{1,0:T(8,128)S(1)} %get-tuple-element.14.refs_1_) | copy-start | bytes 786436
  46.2 0.7 %copy-start.3 = (bf16[256,256]{1,0:T(8,128)(2,1)}, bf16[256,256]{1,0:T(8,128)(2,1)S(1)}, u32[]{:S(2)}) copy-start(bf16[256,256]{1,0:T(8,128)(2,1)S(1)} %get-tuple-element.13.refs_0_) | copy-start | bytes 393220
  46.8 0.7 %copy-start.4 = (bf16[256,256]{1,0:T(8,128)(2,1)}, bf16[256,256]{1,0:T(8,128)(2,1)S(1)}, u32[]{:S(2)}) copy-start(bf16[256,256]{1,0:T(8,128)(2,1)S(1)} %get-tuple-element.15.refs_2_) | copy-start | bytes 393220

commit v3 on v2

--- a/solution.py
+++ b/solution.py
@@ -92,12 +92,13 @@
                     lax.while_loop(lambda position: position >= 0, add, others[place])
                     spot[...] = total[...].astype(BF16)
 
-        rows = pl.ds(row * size, size)
-        if row == 0:
-            feat_copy.wait()
-        partial[rows, :] = jnp.dot(
-            block[rows, :], source[...], preferred_element_type=F32
-        ).astype(BF16)
+        if row % 2 == 1:
+            if row == 1:
+                feat_copy.wait()
+            rows = pl.ds((row - 1) * size, 2 * size)
+            partial[rows, :] = jnp.dot(
+                block[rows, :], source[...], preferred_element_type=F32
+            ).astype(BF16)
 
 
 def block_product(tiles, slots, count, feats):
@@ -131,28 +132,6 @@
     )(slots, count, tiles, feats)
 
 
-def publish_kernel(*refs):
-    number = len(refs) // 2
-    sem = refs[-1]
-    copies = [
-        pltpu.make_async_copy(refs[i], refs[number + i], sem.at[i]) for i in range(number)
-    ]
-    for copy in copies:
-        copy.start()
-    for copy in copies:
-        copy.wait()
-
-
-def publish(*results):
-    return pl.pallas_call(
-        publish_kernel,
-        out_shape=tuple(jax.ShapeDtypeStruct(r.shape, r.dtype) for r in results),
-        in_specs=[pl.BlockSpec(memory_space=pltpu.VMEM)] * len(results),
-        out_specs=tuple(pl.BlockSpec(memory_space=pltpu.HBM) for _ in results),
-        scratch_shapes=[pltpu.SemaphoreType.DMA((len(results),))],
-    )(*results)
-
-
 def remote(src, dst, send_sem, recv_sem, device):
     return pltpu.make_async_remote_copy(
         src_ref=src, dst_ref=dst, send_sem=send_sem, recv_sem=recv_sem,
@@ -163,7 +142,7 @@
 def exchange_kernel(n_row, n_col, scale, block, partial, weight, out_grad,
                     activated, weight_grad, window_grad,
                     core_in, pair_out, pair_in, grads, grads_wide, cross_out, cross_in,
-                    chain_out, chain_in, total, ready, local, piece_in, piece, step_in, whole,
+                    chain_out, chain_in, total, ready, local, local_out, piece_in, piece, step_in, whole,
                     core_sem, pair_sem, own_sem, far_sem, pass_sem, cross_sem,
                     chain_sem, piece_sem, step_sem, whole_sem):
     n_z, n_y = n_row // 2, n_col // 2
@@ -181,7 +160,7 @@
     mirror = (z * 2 + 1 - x, col)
     col_peers = [(row, (col + d) % n_col) for d in range(1, n_col)]
     swaps = []
-    for s in list(range(1, steps)) + [0]:
+    for s in range(steps):
         bit = 1 << s
         swaps.append((row + bit - row // bit % 2 * 2 * bit, col))
     ring = [((row + 2) % n_row, col), ((row + n_row - 2) % n_row, col)]
@@ -259,12 +238,6 @@
         else:
             local[...] += outer
 
-    piece_copies = []
-    for d in range(1, n_col):
-        piece_copies.append(send(
-            local.at[rows_of((col + d) % n_col, depth)], piece_in.at[d - 1],
-            piece_sem.at[0, d - 1], piece_sem.at[1, d - 1], col_peers[d - 1]))
-
     pass_copies = []
     for part in range(PARTS):
         for d in range(1, n_y):
@@ -272,6 +245,12 @@
             got = grads.at[(y + n_y - d) % n_y * 2 + core, part]
             pass_copies.append(send(
                 got, got, pass_sem.at[0, d - 1, part], pass_sem.at[1, d - 1, part], sibling))
+    local_out[...] = local[...].astype(BF16)
+    piece_copies = []
+    for d in range(1, n_col):
+        piece_copies.append(send(
+            local_out.at[rows_of((col + d) % n_col, depth)], piece_in.at[d - 1],
+            piece_sem.at[0, d - 1], piece_sem.at[1, d - 1], col_peers[d - 1]))
     for copy in own_copies + pass_copies:
         copy.wait_recv()
     for owner in range(n_col):
@@ -312,12 +291,6 @@
         return (cross_out.at[at, rows], cross_in.at[at, rows],
                 cross_sem.at[0, at, part], cross_sem.at[1, at, part], mirror)
 
-    for i in range(n_z):
-        at = order(i)
-        cross_out[at] = product(at * 2 + 1 - x).astype(BF16)
-        for part in range(PARTS):
-            send(*cross_copy(at, part))
-
     swap_copies, whole_copies = [], []
 
     def next_swap(s):
@@ -326,17 +299,17 @@
             for copy in piece_copies:
                 copy.wait_recv()
             for d in range(1, n_col):
-                added = added + piece_in[d - 1]
+                added = added + piece_in[d - 1].astype(F32)
         elif s <= steps:
             swap_copies[s - 1].wait_recv()
-            added = piece[s - 1] + step_in[s - 1]
+            added = piece[s - 1].astype(F32) + step_in[s - 1].astype(F32)
         if s < steps:
-            piece[s] = added
+            piece[s] = added.astype(BF16)
             swap_copies.append(send(
                 piece.at[s], step_in.at[s], step_sem.at[0, s], step_sem.at[1, s], swaps[s]))
         elif s == steps:
             spot = whole.at[rows_of(col, depth)]
-            spot[...] = added * scale
+            spot[...] = (added * scale).astype(BF16)
             for d in range(1, n_col):
                 whole_copies.append(send(
                     spot, spot, whole_sem.at[0, d - 1], whole_sem.at[1, d - 1],
@@ -355,7 +328,13 @@
                chain_sem.at[0, up, at, part], chain_sem.at[1, up, at, part], mirror).wait_recv()
         total[rows, :] += chain_in[up, at, rows, :].astype(F32)
 
-    next_swap(0)
+    for i in range(n_z):
+        at = order(i)
+        cross_out[at] = product(at * 2 + 1 - x).astype(BF16)
+        for part in range(PARTS):
+            send(*cross_copy(at, part))
+        if i == 0:
+            next_swap(0)
     for i in range(n_z):
         at = order(i)
         total[...] = product(at * 2 + x)
@@ -383,7 +362,7 @@
         next_swap(s)
     for copy in whole_copies:
         copy.wait_recv()
-    weight_grad[...] = whole[...]
+    weight_grad[...] = whole[...].astype(F32)
     for copy in started:
         copy.wait_send()
     for i in range(n_z - 1):
@@ -426,10 +405,11 @@
             pltpu.VMEM(chunk, F32),
             pltpu.VMEM((window if narrow else 8, width), F32),
             pltpu.VMEM((width, width), F32),
-            pltpu.VMEM((n_col - 1, depth, width), F32),
-            pltpu.VMEM((steps, depth, width), F32),
-            pltpu.VMEM((steps, depth, width), F32),
-            pltpu.VMEM((width, width), F32),
+            pltpu.VMEM((width, width), BF16),
+            pltpu.VMEM((n_col - 1, depth, width), BF16),
+            pltpu.VMEM((steps, depth, width), BF16),
+            pltpu.VMEM((steps, depth, width), BF16),
+            pltpu.VMEM((width, width), BF16),
             dma((2, n_y, PARTS)),
             dma((2, n_y - 1, PARTS)),
             dma((2, PARTS)),
@@ -456,7 +436,6 @@
     activated, weight_grad, window_grad = exchange(
         n_row, n_col, block, partial, weight, out_grad
     )
-    activated, weight_grad, window_grad = publish(activated, weight_grad, window_grad)
     return activated, weight_grad, window_grad[None]
 
 

time: 49.5 us -> 45.5 us (0.919)
  Pallas kernels: 46 us -> 41.8 us
    pallas_call x1, Pallas kernels: 39 us -> 36.5 us  [exchange(): pl.pallas_call(functools.partial(exchange_kernel, n_row, n_col, 1.0 / mat...]
    pallas_call x1 -> x0, Pallas kernels: 1.85 us -> none  [publish(): pl.pallas_call(publish_kernel, out_shape=tuple((jax.ShapeDtypeStruct(r.sh...]
    unnamed x10 -> x7, local copies, waits for them, and re-layouts: 2 us -> 2.02 us
where the time goes in v3:
time: 45.5 us; the launch traced here: 45.2 us
  Pallas kernels  41.8 us (92%)
  local copies, waits for them, and re-layouts  2.02 us (4%)
  between operations  1.37 us (3%)
    pallas_call x1, Pallas kernels, exchange(): pl.pallas_call(functools.partial(exchange_kernel, n_row, n_col, 1.0 / mat...  36.5 us
    pallas_call x1, Pallas kernels, block_product(): pl.pallas_call(block_kernel, out_shape=(jax.ShapeDtypeStruct((RT * size,...  5.28 us
    unnamed x7, local copies, waits for them, and re-layouts  2.02 us

profile of v3, /device:TPU:0, one launch (start us, length us, event | category | flops | bytes accessed | tf_op | source)
XLA Modules:
  0.0 45.2 jit_solution(13950632201058746566)
XLA Ops:
  0.6 0.0 copy-start.1
  0.6 0.0 copy-start
  1.3 5.3 %shard_map.85 = (bf16[1024,2048]{1,0:T(8,128)(2,1)S(1)}, bf16[1024,256]{1,0:T(8,128)(2,1)S(1)}) custom-call(s32[1,24]{1,0:T(1,128)} %slot_list.1, s32[1,1]{1,0:T(1,128)S(6)} %copy.12.live_count, bf16[24,256,256]{2,1,0:T(8,128)(2,1)} %bitcast.3, bf16[2048,256]{1,0:T(8,128)(2,1)} %feats.1), custom_call_target="tpu_custom_call" | custom-call | tf_op jit(solution)/shard_map/pallas_call | solution.py:110
  6.6 0.0 copy-done.1
  6.6 0.0 copy-done
  6.7 36.5 %shard_map.86 = (bf16[256,256]{1,0:T(8,128)(2,1)S(1)}, f32[256,256]{1,0:T(8,128)S(1)}, bf16[256,256]{1,0:T(8,128)(2,1)S(1)}) custom-call(bf16[1024,2048]{1,0:T(8,128)(2,1)S(1)} %get-tuple-element.8.block, bf16[1024,256]{1,0:T(8,128)(2,1)S(1)} %get-tuple-element.9.partial, bf16[256,256]{1,0:T(8,128)(2,1)S(1)} %copy-done, bf16[256,256]{1,0:T(8,128)(2,1)S(1)} %copy-done.1), custom_call_target="tpu_custom_call" | custom-call | tf_op jit(solution)/shard_map/pallas_call | solution.py:386
  43.2 0.7 %copy.13 = bf16[256,256]{1,0:T(8,128)(2,1)} copy(bf16[256,256]{1,0:T(8,128)(2,1)S(1)} %get-tuple-element.16) | data formatting | bytes 262144
  43.9 0.7 %copy.14 = f32[256,256]{1,0:T(8,128)} copy(f32[256,256]{1,0:T(8,128)S(1)} %get-tuple-element.17) | data formatting | bytes 524288
  44.6 0.7 %copy.15 = bf16[1,256,256]{2,1,0:T(8,128)(2,1)} copy(bf16[1,256,256]{2,1,0:T(8,128)(2,1)S(1)} %bitcast.2) | data formatting | bytes 262144
Async XLA Ops:
  0.6 6.0 %copy-start.1 = (bf16[256,256]{1,0:T(8,128)(2,1)S(1)}, bf16[256,256]{1,0:T(8,128)(2,1)}, u32[]{:S(2)}) copy-start(bf16[256,256]{1,0:T(8,128)(2,1)} %out_grad.1) | copy-start | bytes 393220
  0.6 6.0 %copy-start = (bf16[256,256]{1,0:T(8,128)(2,1)S(1)}, bf16[256,256]{1,0:T(8,128)(2,1)}, u32[]{:S(2)}) copy-start(bf16[256,256]{1,0:T(8,128)(2,1)} %weight.1) | copy-start | bytes 393220

commit v4 on v3

--- a/solution.py
+++ b/solution.py
@@ -16,18 +16,14 @@
 BF16 = jnp.bfloat16
 
 
-def block_kernel(slot_list, live_count, tiles, feats, block, partial, extra, source, total,
-                 slots, count, first, others, following, list_sem, tile_sem, feat_sem):
+def block_kernel(slot_list, count, tiles, feats, block, partial, extra, source, total,
+                 slots, first, others, following, list_sem, tile_sem, feat_sem):
     size = tiles.shape[1]
     col_tiles = feats.shape[0] // size
     places = RT * col_tiles
 
-    list_copies = [
-        pltpu.make_async_copy(slot_list, slots, list_sem.at[0]),
-        pltpu.make_async_copy(live_count, count, list_sem.at[1]),
-    ]
-    for copy in list_copies:
-        copy.start()
+    list_copy = pltpu.make_async_copy(slot_list, slots, list_sem)
+    list_copy.start()
     feat_copy = pltpu.make_async_copy(feats, source, feat_sem)
     feat_copy.start()
 
@@ -39,8 +35,7 @@
     for place in range(places):
         first[place] = -1
         others[place] = -1
-    for copy in list_copies:
-        copy.wait()
+    list_copy.wait()
     live = count[0, 0]
 
     @pl.loop(0, live)
@@ -113,18 +108,17 @@
             jax.ShapeDtypeStruct((RT * size, window), BF16),
             jax.ShapeDtypeStruct((RT * size, width), BF16),
         ),
-        in_specs=[hbm, hbm, hbm, hbm],
+        in_specs=[hbm, pl.BlockSpec(memory_space=pltpu.SMEM), hbm, hbm],
         out_specs=(vmem, vmem),
         scratch_shapes=[
             pltpu.VMEM((number, size, size), BF16),
             pltpu.VMEM((window, width), BF16),
             pltpu.VMEM((size, size), F32),
             pltpu.SMEM(slots.shape, jnp.int32),
-            pltpu.SMEM(count.shape, jnp.int32),
             pltpu.SMEM((places,), jnp.int32),
             pltpu.SMEM((places,), jnp.int32),
             pltpu.SMEM((number,), jnp.int32),
-            pltpu.SemaphoreType.DMA((2,)),
+            pltpu.SemaphoreType.DMA,
             pltpu.SemaphoreType.DMA((number,)),
             pltpu.SemaphoreType.DMA,
         ],
@@ -132,11 +126,38 @@
     )(slots, count, tiles, feats)
 
 
+def publish_kernel(*refs):
+    number = len(refs) // 2
+    sem = refs[-1]
+    copies = [
+        pltpu.make_async_copy(refs[i], refs[number + i], sem.at[i]) for i in range(number)
+    ]
+    for copy in copies:
+        copy.start()
+    for copy in copies:
+        copy.wait()
+
+
+def publish(*results):
+    held = [pltpu.with_memory_space_constraint(r, pltpu.VMEM) for r in results]
+    return pl.pallas_call(
+        publish_kernel,
+        out_shape=tuple(jax.ShapeDtypeStruct(r.shape, r.dtype) for r in results),
+        in_specs=[pl.BlockSpec(memory_space=pltpu.VMEM)] * len(results),
+        out_specs=tuple(pl.BlockSpec(memory_space=pltpu.HBM) for _ in results),
+        scratch_shapes=[pltpu.SemaphoreType.DMA((len(results),))],
+    )(*held)
+
+
 def remote(src, dst, send_sem, recv_sem, device):
     return pltpu.make_async_remote_copy(
         src_ref=src, dst_ref=dst, send_sem=send_sem, recv_sem=recv_sem,
         device_id=device, device_id_type=MESH,
     )
+
+
+def slabs_of(rows):
+    return 4 if rows % 64 == 0 else 2
 
 
 def exchange_kernel(n_row, n_col, scale, block, partial, weight, out_grad,
@@ -284,7 +305,8 @@
         at = early * (n_z - 1 - i) + (1 - early) * late
         return at + high * (n_z - 1 - 2 * at)
 
-    slab = total.shape[0] // PARTS
+    slabs = slabs_of(total.shape[0])
+    slab = total.shape[0] // slabs
 
     def cross_copy(at, part):
         rows = pl.ds(part * slab, slab)
@@ -331,14 +353,14 @@
     for i in range(n_z):
         at = order(i)
         cross_out[at] = product(at * 2 + 1 - x).astype(BF16)
-        for part in range(PARTS):
+        for part in range(slabs):
             send(*cross_copy(at, part))
         if i == 0:
             next_swap(0)
     for i in range(n_z):
         at = order(i)
         total[...] = product(at * 2 + x)
-        for part in range(PARTS):
+        for part in range(slabs):
             rows = pl.ds(part * slab, slab)
             remote(*cross_copy(at, part)).wait_recv()
             total[rows, :] += cross_in[at, rows, :].astype(F32)
@@ -366,7 +388,7 @@
     for copy in started:
         copy.wait_send()
     for i in range(n_z - 1):
-        for part in range(PARTS):
+        for part in range(slabs):
             chain_copy(order(i), part).wait_send()
 
 
@@ -381,6 +403,7 @@
     cut = share // PARTS
     narrow = span % LANES != 0
     chunk = (span, width) if narrow else (width, span)
+    slabs = slabs_of(chunk[0])
     dma = pltpu.SemaphoreType.DMA
     vmem = pl.BlockSpec(memory_space=pltpu.VMEM)
     return pl.pallas_call(
@@ -415,8 +438,8 @@
             dma((2, PARTS)),
             dma((2, n_y - 1, PARTS)),
             dma((2, n_y - 1, PARTS)),
-            dma((2, n_z, PARTS)),
-            dma((2, 2, n_z, PARTS)),
+            dma((2, n_z, slabs)),
+            dma((2, 2, n_z, slabs)),
             dma((2, n_col - 1)),
             dma((2, steps)),
             dma((2, n_col - 1)),
@@ -436,6 +459,7 @@
     activated, weight_grad, window_grad = exchange(
         n_row, n_col, block, partial, weight, out_grad
     )
+    activated, weight_grad, window_grad = publish(activated, weight_grad, window_grad)
     return activated, weight_grad, window_grad[None]
 
 

time: 45.5 us -> 43.3 us (0.952)
  local copies, waits for them, and re-layouts: 2.02 us -> 0.01 us
    unnamed x7 -> x4, local copies, waits for them, and re-layouts: 2.02 us -> 0.01 us
    pallas_call x0 -> x1, Pallas kernels: none -> 0.81 us  [publish(): pl.pallas_call(publish_kernel, out_shape=tuple((jax.ShapeDtypeStruct(r.sh...]
    pallas_call x1, Pallas kernels: 36.5 us -> 35.7 us  [exchange(): pl.pallas_call(functools.partial(exchange_kernel, n_row, n_col, 1.0 / mat...]
where the time goes in v4:
time: 43.3 us; the launch traced here: 43 us
  Pallas kernels  41.6 us (96%)
  between operations  1.37 us (3%)
    pallas_call x1, Pallas kernels, exchange(): pl.pallas_call(functools.partial(exchange_kernel, n_row, n_col, 1.0 / mat...  35.7 us
    pallas_call x1, Pallas kernels, block_product(): pl.pallas_call(block_kernel, out_shape=(jax.ShapeDtypeStruct((RT * size,...  5.03 us

profile of v4, /device:TPU:0, one launch (start us, length us, event | category | flops | bytes accessed | tf_op | source)
XLA Modules:
  0.0 43.0 jit_solution(11018201885538100155)
XLA Ops:
  0.6 0.0 copy-start.1
  0.6 0.0 copy-start
  1.3 5.0 %shard_map.85 = (bf16[1024,2048]{1,0:T(8,128)(2,1)S(1)}, bf16[1024,256]{1,0:T(8,128)(2,1)S(1)}) custom-call(s32[1,24]{1,0:T(1,128)} %slot_list.1, s32[1,1]{1,0:T(1,128)S(6)} %copy.9.count, bf16[24,256,256]{2,1,0:T(8,128)(2,1)} %bitcast.2, bf16[2048,256]{1,0:T(8,128)(2,1)} %feats.1), custom_call_target="tpu_custom_call" | custom-call | tf_op jit(solution)/shard_map/pallas_call | solution.py:105
  6.4 0.0 copy-done.1
  6.4 0.0 copy-done
  6.4 35.7 %shard_map.86 = (bf16[256,256]{1,0:T(8,128)(2,1)S(1)}, f32[256,256]{1,0:T(8,128)S(1)}, bf16[256,256]{1,0:T(8,128)(2,1)S(1)}) custom-call(bf16[1024,2048]{1,0:T(8,128)(2,1)S(1)} %get-tuple-element.11.block, bf16[1024,256]{1,0:T(8,128)(2,1)S(1)} %get-tuple-element.12.partial, bf16[256,256]{1,0:T(8,128)(2,1)S(1)} %copy-done, bf16[256,256]{1,0:T(8,128)(2,1)S(1)} %copy-done.1), custom_call_target="tpu_custom_call" | custom-call | tf_op jit(solution)/shard_map/pallas_call | solution.py:409
  42.1 0.8 %shard_map.87 = (bf16[256,256]{1,0:T(8,128)(2,1)}, f32[256,256]{1,0:T(8,128)}, bf16[256,256]{1,0:T(8,128)(2,1)}) custom-call(bf16[256,256]{1,0:T(8,128)(2,1)S(1)} %get-tuple-element.13.refs_0_, f32[256,256]{1,0:T(8,128)S(1)} %get-tuple-element.14.refs_1_, bf16[256,256]{1,0:T(8,128)(2,1)S(1)} %get-tuple-element.15.refs_2_), custom_call_target="tpu_custom_call" | custom-call | tf_op jit(solution)/shard_map/pallas_call | solution.py:143
Async XLA Ops:
  0.6 5.8 %copy-start.1 = (bf16[256,256]{1,0:T(8,128)(2,1)S(1)}, bf16[256,256]{1,0:T(8,128)(2,1)}, u32[]{:S(2)}) copy-start(bf16[256,256]{1,0:T(8,128)(2,1)} %out_grad.1) | copy-start | bytes 393220
  0.6 5.8 %copy-start = (bf16[256,256]{1,0:T(8,128)(2,1)S(1)}, bf16[256,256]{1,0:T(8,128)(2,1)}, u32[]{:S(2)}) copy-start(bf16[256,256]{1,0:T(8,128)(2,1)} %weight.1) | copy-start | bytes 393220

commit v5 on v4

--- a/solution.py
+++ b/solution.py
@@ -156,15 +156,12 @@
     )
 
 
-def slabs_of(rows):
-    return 4 if rows % 64 == 0 else 2
-
-
 def exchange_kernel(n_row, n_col, scale, block, partial, weight, out_grad,
                     activated, weight_grad, window_grad,
-                    core_in, pair_out, pair_in, grads, grads_wide, cross_out, cross_in,
+                    core_in, straight_in, pair_out, pair_in, held_aggregated,
+                    held_grad_pre, grads, grads_wide, cross_out, cross_in,
                     chain_out, chain_in, total, ready, local, local_out, piece_in, piece, step_in, whole,
-                    core_sem, pair_sem, own_sem, far_sem, pass_sem, cross_sem,
+                    core_sem, straight_sem, pair_sem, own_sem, far_sem, pass_sem, cross_sem,
                     chain_sem, piece_sem, step_sem, whole_sem):
     n_z, n_y = n_row // 2, n_col // 2
     row, col = lax.axis_index("row"), lax.axis_index("col")
@@ -209,14 +206,25 @@
         return rows_of(owner * PARTS + part, cut)
 
     core_copies = {}
-    for d in list(range(1, n_y)) + [0]:
-        for part in range(PARTS):
-            owner = (y + d) % n_y * 2 + 1 - core
-            core_copies[d, part] = send(
-                partial.at[part_of(owner, part)], core_in.at[d, part],
-                core_sem.at[0, d, part], core_sem.at[1, d, part], sibling)
+
+    def to_sibling(d, part):
+        owner = (y + d) % n_y * 2 + 1 - core
+        core_copies[d, part] = send(
+            partial.at[part_of(owner, part)], core_in.at[d, part],
+            core_sem.at[0, d, part], core_sem.at[1, d, part], sibling)
+
+    for part in range(1, PARTS):
+        for d in range(1, n_y):
+            to_sibling(d, part)
+    for d in range(1, n_y):
+        for k in range(2):
+            owner = (y + d) % n_y * 2 + k
+            send(partial.at[part_of(owner, 0)], straight_in.at[d - 1, core],
+                 straight_sem.at[0, d - 1, k], straight_sem.at[1, d - 1, core], (row, owner))
+    for part in range(PARTS):
+        to_sibling(0, part)
     pair_copies = {}
-    for part in range(PARTS):
+    for part in range(1, PARTS):
         for d in range(1, n_y):
             core_copies[d, part].wait_recv()
             owner = (y + d) % n_y * 2 + core
@@ -227,13 +235,21 @@
                 pair_out.at[d - 1, part], pair_in.at[d - 1, part],
                 pair_sem.at[0, d - 1, part], pair_sem.at[1, d - 1, part], (row, owner))
 
-    far_copies, own_copies = {}, []
+    own_copies = []
     for part in range(PARTS):
+        last = part == PARTS - 1
         core_copies[0, part].wait_recv()
         sums = partial[part_of(col, part), :].astype(F32) + core_in[0, part].astype(F32)
         for d in range(1, n_y):
-            pair_copies[d, part].wait_recv()
-            sums = sums + pair_in[d - 1, part].astype(F32)
+            if part == 0:
+                for k in range(2):
+                    remote(partial.at[part_of(0, 0)], straight_in.at[d - 1, k],
+                           straight_sem.at[0, d - 1, k], straight_sem.at[1, d - 1, k],
+                           sibling).wait_recv()
+                    sums = sums + straight_in[d - 1, k].astype(F32)
+            else:
+                pair_copies[d, part].wait_recv()
+                sums = sums + pair_in[d - 1, part].astype(F32)
         aggregated = sums.astype(BF16)
         pre_act = jnp.dot(aggregated, weight[...], preferred_element_type=F32)
         sigmoid_pre = jax.nn.sigmoid(pre_act)
@@ -246,26 +262,35 @@
         ).astype(BF16)
         mine = grads.at[col, part]
         for d in range(1, n_y):
-            far_copies[d, part] = send(
-                mine, mine, far_sem.at[0, d - 1, part], far_sem.at[1, d - 1, part],
-                (row, (y + d) % n_y * 2 + core))
+            for turn in range(2 if last else 1):
+                k = (core + turn) % 2
+                send(mine, mine, far_sem.at[0, d - 1, part, turn],
+                     far_sem.at[1, d - 1, part, turn], (row, (y + d) % n_y * 2 + k))
         own_copies.append(send(mine, mine, own_sem.at[0, part], own_sem.at[1, part], sibling))
+        held_aggregated[rows, :] = aggregated
+        held_grad_pre[rows, :] = grad_pre
         activated[rows, :] = (pre_act * sigmoid_pre).astype(BF16)
-        outer = lax.dot_general(
-            aggregated, grad_pre, (((0,), (0,)), ((), ())), preferred_element_type=F32
-        )
-        if part == 0:
-            local[...] = outer
-        else:
-            local[...] += outer
+
+    local[...] = lax.dot_general(
+        held_aggregated[...], held_grad_pre[...], (((0,), (0,)), ((), ())),
+        preferred_element_type=F32,
+    )
+
+    def await_far(d, part, turn):
+        got = grads.at[(y + n_y - d) % n_y * 2 + (core + turn) % 2, part]
+        remote(got, got, far_sem.at[0, d - 1, part, turn], far_sem.at[1, d - 1, part, turn],
+               sibling).wait_recv()
+        return got
 
     pass_copies = []
-    for part in range(PARTS):
+    for part in range(PARTS - 1):
         for d in range(1, n_y):
-            far_copies[d, part].wait_recv()
-            got = grads.at[(y + n_y - d) % n_y * 2 + core, part]
+            got = await_far(d, part, 0)
             pass_copies.append(send(
                 got, got, pass_sem.at[0, d - 1, part], pass_sem.at[1, d - 1, part], sibling))
+    for d in range(1, n_y):
+        for turn in range(2):
+            await_far(d, PARTS - 1, turn)
     local_out[...] = local[...].astype(BF16)
     piece_copies = []
     for d in range(1, n_col):
@@ -305,8 +330,7 @@
         at = early * (n_z - 1 - i) + (1 - early) * late
         return at + high * (n_z - 1 - 2 * at)
 
-    slabs = slabs_of(total.shape[0])
-    slab = total.shape[0] // slabs
+    slab = total.shape[0] // PARTS
 
     def cross_copy(at, part):
         rows = pl.ds(part * slab, slab)
@@ -353,14 +377,14 @@
     for i in range(n_z):
         at = order(i)
         cross_out[at] = product(at * 2 + 1 - x).astype(BF16)
-        for part in range(slabs):
+        for part in range(PARTS):
             send(*cross_copy(at, part))
         if i == 0:
             next_swap(0)
     for i in range(n_z):
         at = order(i)
         total[...] = product(at * 2 + x)
-        for part in range(slabs):
+        for part in range(PARTS):
             rows = pl.ds(part * slab, slab)
             remote(*cross_copy(at, part)).wait_recv()
             total[rows, :] += cross_in[at, rows, :].astype(F32)
@@ -388,7 +412,7 @@
     for copy in started:
         copy.wait_send()
     for i in range(n_z - 1):
-        for part in range(slabs):
+        for part in range(PARTS):
             chain_copy(order(i), part).wait_send()
 
 
@@ -403,7 +427,6 @@
     cut = share // PARTS
     narrow = span % LANES != 0
     chunk = (span, width) if narrow else (width, span)
-    slabs = slabs_of(chunk[0])
     dma = pltpu.SemaphoreType.DMA
     vmem = pl.BlockSpec(memory_space=pltpu.VMEM)
     return pl.pallas_call(
@@ -417,8 +440,11 @@
         out_specs=(vmem, vmem, vmem),
         scratch_shapes=[
             pltpu.VMEM((n_y, PARTS, cut, width), BF16),
+            pltpu.VMEM((n_y - 1, 2, cut, width), BF16),
             pltpu.VMEM((n_y - 1, PARTS, cut, width), BF16),
             pltpu.VMEM((n_y - 1, PARTS, cut, width), BF16),
+            pltpu.VMEM((share, width), BF16),
+            pltpu.VMEM((share, width), BF16),
             pltpu.VMEM((n_col, PARTS, width, cut), BF16),
             pltpu.VMEM((width, rows), BF16),
             pltpu.VMEM((n_z, *chunk), BF16),
@@ -434,12 +460,13 @@
             pltpu.VMEM((steps, depth, width), BF16),
             pltpu.VMEM((width, width), BF16),
             dma((2, n_y, PARTS)),
+            dma((2, n_y - 1, 2)),
             dma((2, n_y - 1, PARTS)),
             dma((2, PARTS)),
+            dma((2, n_y - 1, PARTS, 2)),
             dma((2, n_y - 1, PARTS)),
-            dma((2, n_y - 1, PARTS)),
-            dma((2, n_z, slabs)),
-            dma((2, 2, n_z, slabs)),
+            dma((2, n_z, PARTS)),
+            dma((2, 2, n_z, PARTS)),
             dma((2, n_col - 1)),
             dma((2, steps)),
             dma((2, n_col - 1)),

time: 43.3 us -> 45.3 us (1.046)
  Pallas kernels: 41.6 us -> 43.9 us
    pallas_call x1, Pallas kernels: 35.7 us -> 37.5 us  [exchange(): pl.pallas_call(functools.partial(exchange_kernel, n_row, n_col, 1.0 / mat...]
    pallas_call x1, Pallas kernels: 5.03 us -> 5.6 us  [block_product(): pl.pallas_call(block_kernel, out_shape=(jax.ShapeDtypeStruct((RT * size,...]
where the time goes in v5:
time: 45.3 us
  Pallas kernels  43.9 us (97%)
  between operations  1.37 us (3%)
    pallas_call x1, Pallas kernels, exchange(): pl.pallas_call(functools.partial(exchange_kernel, n_row, n_col, 1.0 / mat...  37.5 us
    pallas_call x1, Pallas kernels, block_product(): pl.pallas_call(block_kernel, out_shape=(jax.ShapeDtypeStruct((RT * size,...  5.6 us

profile of v5, /device:TPU:0, one launch (start us, length us, event | category | flops | bytes accessed | tf_op | source)
XLA Modules:
  0.0 45.3 jit_solution(9231902227426992368)
XLA Ops:
  0.6 0.0 copy-start.1
  0.6 0.0 copy-start
  1.3 5.6 %shard_map.85 = (bf16[1024,2048]{1,0:T(8,128)(2,1)S(1)}, bf16[1024,256]{1,0:T(8,128)(2,1)S(1)}) custom-call(s32[1,24]{1,0:T(1,128)} %slot_list.1, s32[1,1]{1,0:T(1,128)S(6)} %copy.9.count, bf16[24,256,256]{2,1,0:T(8,128)(2,1)} %bitcast.2, bf16[2048,256]{1,0:T(8,128)(2,1)} %feats.1), custom_call_target="tpu_custom_call" | custom-call | tf_op jit(solution)/shard_map/pallas_call | solution.py:105
  6.9 0.0 copy-done.1
  7.0 0.0 copy-done
  7.0 37.5 %shard_map.86 = (bf16[256,256]{1,0:T(8,128)(2,1)S(1)}, f32[256,256]{1,0:T(8,128)S(1)}, bf16[256,256]{1,0:T(8,128)(2,1)S(1)}) custom-call(bf16[1024,2048]{1,0:T(8,128)(2,1)S(1)} %get-tuple-element.11.block, bf16[1024,256]{1,0:T(8,128)(2,1)S(1)} %get-tuple-element.12.partial, bf16[256,256]{1,0:T(8,128)(2,1)S(1)} %copy-done, bf16[256,256]{1,0:T(8,128)(2,1)S(1)} %copy-done.1), custom_call_target="tpu_custom_call" | custom-call | tf_op jit(solution)/shard_map/pallas_call | solution.py:432
  44.5 0.8 %shard_map.87 = (bf16[256,256]{1,0:T(8,128)(2,1)}, f32[256,256]{1,0:T(8,128)}, bf16[256,256]{1,0:T(8,128)(2,1)}) custom-call(bf16[256,256]{1,0:T(8,128)(2,1)S(1)} %get-tuple-element.13.refs_0_, f32[256,256]{1,0:T(8,128)S(1)} %get-tuple-element.14.refs_1_, bf16[256,256]{1,0:T(8,128)(2,1)S(1)} %get-tuple-element.15.refs_2_), custom_call_target="tpu_custom_call" | custom-call | tf_op jit(solution)/shard_map/pallas_call | solution.py:143
Async XLA Ops:
  0.6 6.3 %copy-start.1 = (bf16[256,256]{1,0:T(8,128)(2,1)S(1)}, bf16[256,256]{1,0:T(8,128)(2,1)}, u32[]{:S(2)}) copy-start(bf16[256,256]{1,0:T(8,128)(2,1)} %out_grad.1) | copy-start | bytes 393220
  0.6 6.3 %copy-start = (bf16[256,256]{1,0:T(8,128)(2,1)S(1)}, bf16[256,256]{1,0:T(8,128)(2,1)}, u32[]{:S(2)}) copy-start(bf16[256,256]{1,0:T(8,128)(2,1)} %weight.1) | copy-start | bytes 393220

commit v6 on v4

--- a/solution.py
+++ b/solution.py
@@ -163,9 +163,10 @@
 def exchange_kernel(n_row, n_col, scale, block, partial, weight, out_grad,
                     activated, weight_grad, window_grad,
                     core_in, pair_out, pair_in, grads, grads_wide, cross_out, cross_in,
-                    chain_out, chain_in, total, ready, local, local_out, piece_in, piece, step_in, whole,
+                    chain_out, chain_in, total, ready, held_aggregated, held_grad_pre,
+                    local, half_out, half_in, piece_in, piece, step_in, whole,
                     core_sem, pair_sem, own_sem, far_sem, pass_sem, cross_sem,
-                    chain_sem, piece_sem, step_sem, whole_sem):
+                    chain_sem, half_sem, piece_sem, step_sem, whole_sem):
     n_z, n_y = n_row // 2, n_col // 2
     row, col = lax.axis_index("row"), lax.axis_index("col")
     z, x = row // 2, row % 2
@@ -174,14 +175,14 @@
     span = window_grad.shape[0]
     width = weight.shape[0]
     depth = width // n_col
-    steps = n_row.bit_length() - 1
+    steps = n_row.bit_length() - 2
     cut = share // PARTS
 
     sibling = (row, y * 2 + 1 - core)
     mirror = (z * 2 + 1 - x, col)
     col_peers = [(row, (col + d) % n_col) for d in range(1, n_col)]
     swaps = []
-    for s in range(steps):
+    for s in range(steps + 1):
         bit = 1 << s
         swaps.append((row + bit - row // bit % 2 * 2 * bit, col))
     ring = [((row + 2) % n_row, col), ((row + n_row - 2) % n_row, col)]
@@ -250,14 +251,17 @@
                 mine, mine, far_sem.at[0, d - 1, part], far_sem.at[1, d - 1, part],
                 (row, (y + d) % n_y * 2 + core))
         own_copies.append(send(mine, mine, own_sem.at[0, part], own_sem.at[1, part], sibling))
+        held_aggregated[rows, :] = aggregated
+        held_grad_pre[rows, :] = grad_pre
         activated[rows, :] = (pre_act * sigmoid_pre).astype(BF16)
-        outer = lax.dot_general(
-            aggregated, grad_pre, (((0,), (0,)), ((), ())), preferred_element_type=F32
-        )
-        if part == 0:
-            local[...] = outer
-        else:
-            local[...] += outer
+
+    half = width // 2
+    local[...] = lax.dot_general(
+        held_aggregated[...], held_grad_pre[...], (((0,), (0,)), ((), ())),
+        preferred_element_type=F32,
+    )
+    half_out[0] = local[rows_of(1 - core, half), :].astype(BF16)
+    half_copy = send(half_out.at[0], half_in.at[0], half_sem.at[0, 0], half_sem.at[1, 0], sibling)
 
     pass_copies = []
     for part in range(PARTS):
@@ -266,12 +270,9 @@
             got = grads.at[(y + n_y - d) % n_y * 2 + core, part]
             pass_copies.append(send(
                 got, got, pass_sem.at[0, d - 1, part], pass_sem.at[1, d - 1, part], sibling))
-    local_out[...] = local[...].astype(BF16)
-    piece_copies = []
-    for d in range(1, n_col):
-        piece_copies.append(send(
-            local_out.at[rows_of((col + d) % n_col, depth)], piece_in.at[d - 1],
-            piece_sem.at[0, d - 1], piece_sem.at[1, d - 1], col_peers[d - 1]))
+    half_copy.wait_recv()
+    half_out[1] = (local[rows_of(core, half), :] + half_in[0].astype(F32)).astype(BF16)
+    half_copy = send(half_out.at[1], half_in.at[1], half_sem.at[0, 1], half_sem.at[1, 1], mirror)
     for copy in own_copies + pass_copies:
         copy.wait_recv()
     for owner in range(n_col):
@@ -313,14 +314,25 @@
         return (cross_out.at[at, rows], cross_in.at[at, rows],
                 cross_sem.at[0, at, part], cross_sem.at[1, at, part], mirror)
 
-    swap_copies, whole_copies = [], []
+    piece_copies, swap_copies, whole_copies = [], [], []
+    place = core * n_y + y
+
+    def cut_along_y():
+        half_copy.wait_recv()
+        local[pl.ds(0, half), :] = half_out[1].astype(F32) + half_in[1].astype(F32)
+        half_out[2] = local[pl.ds(0, half), :].astype(BF16)
+        for d in range(1, n_y):
+            at = (y + d) % n_y
+            piece_copies.append(send(
+                half_out.at[2, rows_of(at, depth)], piece_in.at[d - 1],
+                piece_sem.at[0, d - 1], piece_sem.at[1, d - 1], (row, at * 2 + core)))
 
     def next_swap(s):
         if s == 0:
-            added = local[rows_of(col, depth), :]
+            added = local[rows_of(y, depth), :]
             for copy in piece_copies:
                 copy.wait_recv()
-            for d in range(1, n_col):
+            for d in range(1, n_y):
                 added = added + piece_in[d - 1].astype(F32)
         elif s <= steps:
             swap_copies[s - 1].wait_recv()
@@ -328,9 +340,9 @@
         if s < steps:
             piece[s] = added.astype(BF16)
             swap_copies.append(send(
-                piece.at[s], step_in.at[s], step_sem.at[0, s], step_sem.at[1, s], swaps[s]))
+                piece.at[s], step_in.at[s], step_sem.at[0, s], step_sem.at[1, s], swaps[s + 1]))
         elif s == steps:
-            spot = whole.at[rows_of(col, depth)]
+            spot = whole.at[rows_of(place, depth)]
             spot[...] = (added * scale).astype(BF16)
             for d in range(1, n_col):
                 whole_copies.append(send(
@@ -355,8 +367,8 @@
         cross_out[at] = product(at * 2 + 1 - x).astype(BF16)
         for part in range(slabs):
             send(*cross_copy(at, part))
-        if i == 0:
-            next_swap(0)
+        if i == min(1, n_z - 1):
+            cut_along_y()
     for i in range(n_z):
         at = order(i)
         total[...] = product(at * 2 + x)
@@ -379,8 +391,8 @@
         if i == n_z - 1:
             result = total[...] if narrow else total[...].T
             window_grad[...] = result.astype(BF16)
-        next_swap(i + 1)
-    for s in range(n_z + 1, steps + 1):
+        next_swap(i)
+    for s in range(n_z, steps + 1):
         next_swap(s)
     for copy in whole_copies:
         copy.wait_recv()
@@ -399,7 +411,7 @@
     span = window // n_row
     n_z, n_y = n_row // 2, n_col // 2
     depth = width // n_col
-    steps = n_row.bit_length() - 1
+    steps = n_row.bit_length() - 2
     cut = share // PARTS
     narrow = span % LANES != 0
     chunk = (span, width) if narrow else (width, span)
@@ -427,9 +439,12 @@
             pltpu.VMEM((2, n_z, *chunk), BF16),
             pltpu.VMEM(chunk, F32),
             pltpu.VMEM((window if narrow else 8, width), F32),
+            pltpu.VMEM((share, width), BF16),
+            pltpu.VMEM((share, width), BF16),
             pltpu.VMEM((width, width), F32),
-            pltpu.VMEM((width, width), BF16),
-            pltpu.VMEM((n_col - 1, depth, width), BF16),
+            pltpu.VMEM((3, width // 2, width), BF16),
+            pltpu.VMEM((2, width // 2, width), BF16),
+            pltpu.VMEM((n_y - 1, depth, width), BF16),
             pltpu.VMEM((steps, depth, width), BF16),
             pltpu.VMEM((steps, depth, width), BF16),
             pltpu.VMEM((width, width), BF16),
@@ -440,7 +455,8 @@
             dma((2, n_y - 1, PARTS)),
             dma((2, n_z, slabs)),
             dma((2, 2, n_z, slabs)),
-            dma((2, n_col - 1)),
+            dma((2, 2)),
+            dma((2, n_y - 1)),
             dma((2, steps)),
             dma((2, n_col - 1)),
         ],

time: 43.3 us -> 43.8 us (1.012)
  Pallas kernels: 41.6 us -> 42.4 us
    pallas_call x1, Pallas kernels: 5.03 us -> 5.87 us  [block_product(): pl.pallas_call(block_kernel, out_shape=(jax.ShapeDtypeStruct((RT * size,...]
where the time goes in v6:
time: 43.8 us
  Pallas kernels  42.4 us (97%)
  between operations  1.37 us (3%)
    pallas_call x1, Pallas kernels, exchange(): pl.pallas_call(functools.partial(exchange_kernel, n_row, n_col, 1.0 / mat...  35.7 us
    pallas_call x1, Pallas kernels, block_product(): pl.pallas_call(block_kernel, out_shape=(jax.ShapeDtypeStruct((RT * size,...  5.87 us

profile of v6, /device:TPU:0, one launch (start us, length us, event | category | flops | bytes accessed | tf_op | source)
XLA Modules:
  0.0 43.8 jit_solution(8733642551561919496)
XLA Ops:
  0.6 0.0 copy-start.1
  0.6 0.0 copy-start
  1.3 5.9 %shard_map.85 = (bf16[1024,2048]{1,0:T(8,128)(2,1)S(1)}, bf16[1024,256]{1,0:T(8,128)(2,1)S(1)}) custom-call(s32[1,24]{1,0:T(1,128)} %slot_list.1, s32[1,1]{1,0:T(1,128)S(6)} %copy.9.count, bf16[24,256,256]{2,1,0:T(8,128)(2,1)} %bitcast.2, bf16[2048,256]{1,0:T(8,128)(2,1)} %feats.1), custom_call_target="tpu_custom_call" | custom-call | tf_op jit(solution)/shard_map/pallas_call | solution.py:105
  7.2 0.0 copy-done.1
  7.2 0.0 copy-done
  7.2 35.7 %shard_map.86 = (bf16[256,256]{1,0:T(8,128)(2,1)S(1)}, f32[256,256]{1,0:T(8,128)S(1)}, bf16[256,256]{1,0:T(8,128)(2,1)S(1)}) custom-call(bf16[1024,2048]{1,0:T(8,128)(2,1)S(1)} %get-tuple-element.11.block, bf16[1024,256]{1,0:T(8,128)(2,1)S(1)} %get-tuple-element.12.partial, bf16[256,256]{1,0:T(8,128)(2,1)S(1)} %copy-done, bf16[256,256]{1,0:T(8,128)(2,1)S(1)} %copy-done.1), custom_call_target="tpu_custom_call" | custom-call | tf_op jit(solution)/shard_map/pallas_call | solution.py:421
  43.0 0.8 %shard_map.87 = (bf16[256,256]{1,0:T(8,128)(2,1)}, f32[256,256]{1,0:T(8,128)}, bf16[256,256]{1,0:T(8,128)(2,1)}) custom-call(bf16[256,256]{1,0:T(8,128)(2,1)S(1)} %get-tuple-element.13.refs_0_, f32[256,256]{1,0:T(8,128)S(1)} %get-tuple-element.14.refs_1_, bf16[256,256]{1,0:T(8,128)(2,1)S(1)} %get-tuple-element.15.refs_2_), custom_call_target="tpu_custom_call" | custom-call | tf_op jit(solution)/shard_map/pallas_call | solution.py:143
Async XLA Ops:
  0.6 6.6 %copy-start.1 = (bf16[256,256]{1,0:T(8,128)(2,1)S(1)}, bf16[256,256]{1,0:T(8,128)(2,1)}, u32[]{:S(2)}) copy-start(bf16[256,256]{1,0:T(8,128)(2,1)} %out_grad.1) | copy-start | bytes 393220
  0.6 6.6 %copy-start = (bf16[256,256]{1,0:T(8,128)(2,1)S(1)}, bf16[256,256]{1,0:T(8,128)(2,1)}, u32[]{:S(2)}) copy-start(bf16[256,256]{1,0:T(8,128)(2,1)} %weight.1) | copy-start | bytes 393220

commit v7 on v6

--- a/solution.py
+++ b/solution.py
@@ -35,6 +35,7 @@
     for place in range(places):
         first[place] = -1
         others[place] = -1
+    block[...] = jnp.zeros_like(block)
     list_copy.wait()
     live = count[0, 0]
 
@@ -55,12 +56,6 @@
             pltpu.make_async_copy(
                 tiles.at[position], extra.at[position], tile_sem.at[position]
             ).start()
-
-    @pl.loop(0, places)
-    def _(place):
-        @pl.when(first[place] < 0)
-        def _():
-            place_of(place)[...] = jnp.zeros((size, size), BF16)
 
     def await_tile(position):
         pltpu.make_async_copy(

time: 43.8 us -> 44.1 us (level)
    pallas_call x1, Pallas kernels: 35.7 us -> 36.8 us  [exchange(): pl.pallas_call(functools.partial(exchange_kernel, n_row, n_col, 1.0 / mat...]
    pallas_call x1, Pallas kernels: 5.87 us -> 4.93 us  [block_product(): pl.pallas_call(block_kernel, out_shape=(jax.ShapeDtypeStruct((RT * size,...]
where the time goes in v7:
time: 44.1 us; the launch traced here: 43.9 us
  Pallas kernels  42.5 us (96%)
  between operations  1.37 us (3%)
    pallas_call x1, Pallas kernels, exchange(): pl.pallas_call(functools.partial(exchange_kernel, n_row, n_col, 1.0 / mat...  36.8 us
    pallas_call x1, Pallas kernels, block_product(): pl.pallas_call(block_kernel, out_shape=(jax.ShapeDtypeStruct((RT * size,...  4.93 us

profile of v7, /device:TPU:0, one launch (start us, length us, event | category | flops | bytes accessed | tf_op | source)
XLA Modules:
  0.0 43.9 jit_solution(11296302666848416433)
XLA Ops:
  0.6 0.0 copy-start.1
  0.6 0.0 copy-start
  1.3 4.9 %shard_map.85 = (bf16[1024,2048]{1,0:T(8,128)(2,1)S(1)}, bf16[1024,256]{1,0:T(8,128)(2,1)S(1)}) custom-call(s32[1,24]{1,0:T(1,128)} %slot_list.1, s32[1,1]{1,0:T(1,128)S(6)} %copy.9.count, bf16[24,256,256]{2,1,0:T(8,128)(2,1)} %bitcast.2, bf16[2048,256]{1,0:T(8,128)(2,1)} %feats.1), custom_call_target="tpu_custom_call" | custom-call | tf_op jit(solution)/shard_map/pallas_call | solution.py:100
  6.3 0.0 copy-done.1
  6.3 0.0 copy-done
  6.3 36.8 %shard_map.86 = (bf16[256,256]{1,0:T(8,128)(2,1)S(1)}, f32[256,256]{1,0:T(8,128)S(1)}, bf16[256,256]{1,0:T(8,128)(2,1)S(1)}) custom-call(bf16[1024,2048]{1,0:T(8,128)(2,1)S(1)} %get-tuple-element.11.block, bf16[1024,256]{1,0:T(8,128)(2,1)S(1)} %get-tuple-element.12.partial, bf16[256,256]{1,0:T(8,128)(2,1)S(1)} %copy-done, bf16[256,256]{1,0:T(8,128)(2,1)S(1)} %copy-done.1), custom_call_target="tpu_custom_call" | custom-call | tf_op jit(solution)/shard_map/pallas_call | solution.py:416
  43.1 0.8 %shard_map.87 = (bf16[256,256]{1,0:T(8,128)(2,1)}, f32[256,256]{1,0:T(8,128)}, bf16[256,256]{1,0:T(8,128)(2,1)}) custom-call(bf16[256,256]{1,0:T(8,128)(2,1)S(1)} %get-tuple-element.13.refs_0_, f32[256,256]{1,0:T(8,128)S(1)} %get-tuple-element.14.refs_1_, bf16[256,256]{1,0:T(8,128)(2,1)S(1)} %get-tuple-element.15.refs_2_), custom_call_target="tpu_custom_call" | custom-call | tf_op jit(solution)/shard_map/pallas_call | solution.py:138
Async XLA Ops:
  0.6 5.7 %copy-start.1 = (bf16[256,256]{1,0:T(8,128)(2,1)S(1)}, bf16[256,256]{1,0:T(8,128)(2,1)}, u32[]{:S(2)}) copy-start(bf16[256,256]{1,0:T(8,128)(2,1)} %out_grad.1) | copy-start | bytes 393220
  0.6 5.7 %copy-start = (bf16[256,256]{1,0:T(8,128)(2,1)S(1)}, bf16[256,256]{1,0:T(8,128)(2,1)}, u32[]{:S(2)}) copy-start(bf16[256,256]{1,0:T(8,128)(2,1)} %weight.1) | copy-start | bytes 393220

commit v8 on v4

--- a/solution.py
+++ b/solution.py
@@ -355,7 +355,7 @@
         cross_out[at] = product(at * 2 + 1 - x).astype(BF16)
         for part in range(slabs):
             send(*cross_copy(at, part))
-        if i == 0:
+        if i == min(1, n_z - 1):
             next_swap(0)
     for i in range(n_z):
         at = order(i)

time: 43.3 us -> 44.1 us (1.018); the launches traced: 43 us -> 43.3 us
    pallas_call x1, Pallas kernels: 35.7 us -> 36.3 us  [exchange(): pl.pallas_call(functools.partial(exchange_kernel, n_row, n_col, 1.0 / mat...]
where the time goes in v8:
time: 44.1 us; the launch traced here: 43.3 us
  Pallas kernels  41.9 us (95%)
  between operations  1.37 us (3%)
    pallas_call x1, Pallas kernels, exchange(): pl.pallas_call(functools.partial(exchange_kernel, n_row, n_col, 1.0 / mat...  36.3 us
    pallas_call x1, Pallas kernels, block_product(): pl.pallas_call(block_kernel, out_shape=(jax.ShapeDtypeStruct((RT * size,...  4.77 us

profile of v8, /device:TPU:0, one launch (start us, length us, event | category | flops | bytes accessed | tf_op | source)
XLA Modules:
  0.0 43.3 jit_solution(14206086019349365754)
XLA Ops:
  0.6 0.0 copy-start.1
  0.6 0.0 copy-start
  1.3 4.8 %shard_map.85 = (bf16[1024,2048]{1,0:T(8,128)(2,1)S(1)}, bf16[1024,256]{1,0:T(8,128)(2,1)S(1)}) custom-call(s32[1,24]{1,0:T(1,128)} %slot_list.1, s32[1,1]{1,0:T(1,128)S(6)} %copy.9.count, bf16[24,256,256]{2,1,0:T(8,128)(2,1)} %bitcast.2, bf16[2048,256]{1,0:T(8,128)(2,1)} %feats.1), custom_call_target="tpu_custom_call" | custom-call | tf_op jit(solution)/shard_map/pallas_call | solution.py:105
  6.1 0.0 copy-done.1
  6.1 0.0 copy-done
  6.1 36.3 %shard_map.86 = (bf16[256,256]{1,0:T(8,128)(2,1)S(1)}, f32[256,256]{1,0:T(8,128)S(1)}, bf16[256,256]{1,0:T(8,128)(2,1)S(1)}) custom-call(bf16[1024,2048]{1,0:T(8,128)(2,1)S(1)} %get-tuple-element.11.block, bf16[1024,256]{1,0:T(8,128)(2,1)S(1)} %get-tuple-element.12.partial, bf16[256,256]{1,0:T(8,128)(2,1)S(1)} %copy-done, bf16[256,256]{1,0:T(8,128)(2,1)S(1)} %copy-done.1), custom_call_target="tpu_custom_call" | custom-call | tf_op jit(solution)/shard_map/pallas_call | solution.py:409
  42.5 0.8 %shard_map.87 = (bf16[256,256]{1,0:T(8,128)(2,1)}, f32[256,256]{1,0:T(8,128)}, bf16[256,256]{1,0:T(8,128)(2,1)}) custom-call(bf16[256,256]{1,0:T(8,128)(2,1)S(1)} %get-tuple-element.13.refs_0_, f32[256,256]{1,0:T(8,128)S(1)} %get-tuple-element.14.refs_1_, bf16[256,256]{1,0:T(8,128)(2,1)S(1)} %get-tuple-element.15.refs_2_), custom_call_target="tpu_custom_call" | custom-call | tf_op jit(solution)/shard_map/pallas_call | solution.py:143
Async XLA Ops:
  0.6 5.5 %copy-start.1 = (bf16[256,256]{1,0:T(8,128)(2,1)S(1)}, bf16[256,256]{1,0:T(8,128)(2,1)}, u32[]{:S(2)}) copy-start(bf16[256,256]{1,0:T(8,128)(2,1)} %out_grad.1) | copy-start | bytes 393220
  0.6 5.5 %copy-start = (bf16[256,256]{1,0:T(8,128)(2,1)S(1)}, bf16[256,256]{1,0:T(8,128)(2,1)}, u32[]{:S(2)}) copy-start(bf16[256,256]{1,0:T(8,128)(2,1)} %weight.1) | copy-start | bytes 393220
